TPU v7x, 32 devices: a whole 2x2x4 slice. The times are simulated.
32 devices in a mesh: dp: 4 (over z), sp: 4 (over y, x), tp: 2 (over core).
Axes of the slice: x: 2, y: 2, z: 4, core: 2. Of those that a mesh axis runs over, the one named last changes fastest.
Arguments:
- inputs: bfloat16 [4, 2048, 2048], P('dp', 'sp'), may hold values from -6 to 6
- lengths: int32 [4], P('dp'), may hold values from 512 to 2048, as said below
- first_gain: float32 [2048], replicated, may hold values from 0.5 to 1.5
- first_bias: float32 [2048], replicated, may hold values from -4 to 4
- query_weight: bfloat16 [2048, 2048], P(None, 'tp'), may hold values from -0.1875 to 0.1875
- query_bias: float32 [2048], P('tp'), may hold values from -4 to 4
- keyval_weight: bfloat16 [2048, 256], replicated, may hold values from -0.1875 to 0.1875
- value_bias: float32 [128], replicated, may hold values from -4 to 4
- output_weight: bfloat16 [2048, 2048], P('tp'), may hold values from -0.5 to 0.5
- output_bias: float32 [2048], replicated, may hold values from -4 to 4
- second_gain: float32 [2048], replicated, may hold values from 0.5 to 1.5
- second_bias: float32 [2048], replicated, may hold values from -4 to 4
- up_weight: bfloat16 [2048, 8192], P(None, 'tp'), may hold values from -0.125 to 0.125
- up_bias: float32 [8192], P('tp'), may hold values from -6 to 6
- down_weight: bfloat16 [8192, 2048], P('tp'), may hold values from -0.09375 to 0.09375
- down_bias: float32 [2048], replicated, may hold values from -4 to 4
- cotangent: bfloat16 [4, 2048, 2048], P('dp', 'sp'), may hold values from -6 to 6
Outputs:
- outputs: bfloat16 [4, 2048, 2048], P('dp', 'sp')
- input_grad: bfloat16 [4, 2048, 2048], P('dp', 'sp')
- first_gain_grad: float32 [2048], replicated
- first_bias_grad: float32 [2048], replicated
- query_weight_grad: float32 [2048, 2048], P(('dp', 'sp'), 'tp')
- query_bias_grad: float32 [2048], P('tp')
- keyval_weight_grad: float32 [2048, 256], P(('dp', 'sp'))
- value_bias_grad: float32 [128], replicated
- output_weight_grad: float32 [2048, 2048], P('tp', ('dp', 'sp'))
- output_bias_grad: float32 [2048], replicated
- second_gain_grad: float32 [2048], replicated
- second_bias_grad: float32 [2048], replicated
- up_weight_grad: float32 [2048, 8192], P(('dp', 'sp'), 'tp')
- up_bias_grad: float32 [8192], P('tp')
- down_weight_grad: float32 [8192, 2048], P('tp', ('dp', 'sp'))
- down_bias_grad: float32 [2048], replicated
Inputs may be any that keep to these rules, and one draw needn't show every extreme that they name: Row r's first lengths[r] tokens are real and the others padding; in every draw some row has all 2048 tokens real.
All inputs are finite; a program needn't handle non-finite values.
Results may differ from a plain program's by a relative error of at most 0.019.
Values may be sent and summed in bfloat16 or wider, within the bound.
A program may use at most 320 MiB of HBM per device.

v0:
```python
import math

import jax
import jax.numpy as jnp
from jax import lax
from jax.sharding import PartitionSpec as P

HD = 128
LEN = 2048
GROUPS = 4


EPS = 1e-05


def matmul(left, right):
    return jnp.dot(left, right, preferred_element_type=jnp.float32)


def lead_product(left, right):
    return lax.dot_general(
        left, right, (((0,), (0,)), ((), ())), preferred_element_type=jnp.float32
    )


def tail_product(left, right):
    return lax.dot_general(
        left, right, (((1,), (1,)), ((), ())), preferred_element_type=jnp.float32
    )


def normalize(values, norm_gain, norm_bias):
    average = jnp.mean(values, axis=-1, keepdims=True)
    centered = values - average
    variance = jnp.mean(centered * centered, axis=-1, keepdims=True)
    inv_std = lax.rsqrt(variance + EPS)
    scaled = centered * inv_std
    return (scaled * norm_gain + norm_bias, scaled, inv_std)


def norm_back(gradient, scaled, inv_std, norm_gain):
    inner_term = gradient * norm_gain
    mean_one = jnp.mean(inner_term, axis=-1, keepdims=True)
    mean_two = jnp.mean(inner_term * scaled, axis=-1, keepdims=True)
    back = inv_std * (inner_term - mean_one - scaled * mean_two)
    return (back, jnp.sum(gradient * scaled, axis=0), jnp.sum(gradient, axis=0))


def split_groups(values, row_count, seg_len, groups):
    width = values.shape[1] // groups
    shaped = values.reshape(row_count, seg_len, groups, width).transpose(0, 2, 1, 3)
    return shaped.reshape(row_count * groups, seg_len, width)


def join_groups(values, row_count, seg_len, groups):
    width = values.shape[2]
    shaped = values.reshape(row_count, groups, seg_len, width).transpose(0, 2, 1, 3)
    return shaped.reshape(row_count * seg_len, groups * width)


def block_scores(query_block, keys_part, first, block, length):
    scale_factor = 1.0 / math.sqrt(HD)
    scores = (
        jnp.einsum("qhd,kd->hqk", query_block, keys_part, preferred_element_type=jnp.float32)
        * scale_factor
    )
    query_pos = first + jnp.arange(block, dtype=jnp.int32)
    key_pos = jnp.arange(keys_part.shape[0], dtype=jnp.int32)
    allowed = (key_pos[None, :] <= query_pos[:, None]) & (key_pos[None, :] < length)
    return jnp.where(allowed[None], scores, -1e30)


def attend_forward(query_seq, keyval_seq, length):
    head_count = query_seq.shape[1] // HD
    block = min(512, LEN)
    attended_parts = []
    log_totals = []
    for index in range(LEN // block):
        first = index * block
        block_end = first + block
        query_block = query_seq[first:block_end].reshape(block, head_count, HD)
        scores = block_scores(query_block, keyval_seq[:block_end, :HD], first, block, length)
        top = jnp.max(scores, axis=-1, keepdims=True)
        weights = jnp.exp(scores - top)
        total = jnp.sum(weights, axis=-1, keepdims=True)
        prob = weights / total
        mixed = jnp.einsum(
            "hqk,kd->qhd",
            prob.astype(jnp.bfloat16),
            keyval_seq[:block_end, HD:],
            preferred_element_type=jnp.float32,
        )
        attended_parts.append(mixed.astype(jnp.bfloat16).reshape(block, head_count * HD))
        log_totals.append(top + jnp.log(total))
    return (jnp.concatenate(attended_parts, axis=0), log_totals)


def attend_backward(query_seq, keyval_seq, length, log_totals, dattn_seq):
    head_count = query_seq.shape[1] // HD
    block = min(512, LEN)
    scale_factor = 1.0 / math.sqrt(HD)
    key_grad = jnp.zeros((LEN, HD), jnp.float32)
    value_grad = jnp.zeros((LEN, HD), jnp.float32)
    query_parts = []
    for index in range(LEN // block):
        first = index * block
        block_end = first + block
        query_block = query_seq[first:block_end].reshape(block, head_count, HD)
        keys_part = keyval_seq[:block_end, :HD]
        values_part = keyval_seq[:block_end, HD:]
        scores = block_scores(query_block, keys_part, first, block, length)
        prob = jnp.exp(scores - log_totals[index])
        dattn_block = dattn_seq[first:block_end].reshape(block, head_count, HD)
        dprob = jnp.einsum(
            "qhd,kd->hqk", dattn_block, values_part, preferred_element_type=jnp.float32
        )
        delta = jnp.sum(prob * dprob, axis=-1, keepdims=True)
        dscore = (prob * (dprob - delta)).astype(jnp.bfloat16)
        dquery_block = (
            jnp.einsum("hqk,kd->qhd", dscore, keys_part, preferred_element_type=jnp.float32)
            * scale_factor
        )
        query_parts.append(dquery_block.astype(jnp.bfloat16).reshape(block, head_count * HD))
        key_term = (
            jnp.einsum("hqk,qhd->kd", dscore, query_block, preferred_element_type=jnp.float32)
            * scale_factor
        )
        value_term = jnp.einsum(
            "hqk,qhd->kd",
            prob.astype(jnp.bfloat16),
            dattn_block,
            preferred_element_type=jnp.float32,
        )
        key_grad = key_grad.at[:block_end].add(key_term)
        value_grad = value_grad.at[:block_end].add(value_term)
    return (jnp.concatenate(query_parts, axis=0), jnp.concatenate([key_grad, value_grad], axis=1))


def gelu_tanh(values):
    return jax.nn.gelu(values, approximate=True)


def per_device(
    inputs,
    lengths,
    first_gain,
    first_bias,
    query_weight,
    query_bias,
    keyval_weight,
    value_bias,
    output_weight,
    output_bias,
    second_gain,
    second_bias,
    up_weight,
    up_bias,
    down_weight,
    down_bias,
    cotangent,
):
    row_count, seg_len, width = inputs.shape
    token_count = row_count * seg_len
    groups = GROUPS
    row_pick = lax.axis_index("sp") // groups
    length = lax.dynamic_index_in_dim(lengths, row_pick, 0, keepdims=False)
    flat_inputs = inputs.reshape(token_count, width).astype(jnp.float32)
    norm_one, hat_one, inv_one = normalize(flat_inputs, first_gain, first_bias)
    v_first = norm_one.astype(jnp.bfloat16)
    query = (matmul(v_first, query_weight) + query_bias).astype(jnp.bfloat16)
    kv_bias = jnp.concatenate([jnp.zeros((HD,), jnp.float32), value_bias])
    keyval = (matmul(v_first, keyval_weight) + kv_bias).astype(jnp.bfloat16)
    query_send = split_groups(query, row_count, seg_len, groups)
    keyval_send = jnp.broadcast_to(
        keyval.reshape(row_count, 1, seg_len, 2 * HD), (row_count, groups, seg_len, 2 * HD)
    ).reshape(row_count * groups, seg_len, 2 * HD)
    query_rows, keyval_rows = (
        lax.all_to_all(query_send, "sp", split_axis=0, concat_axis=1, tiled=True),
        lax.all_to_all(keyval_send, "sp", split_axis=0, concat_axis=1, tiled=True),
    )
    query_seq = query_rows[0]
    keyval_seq = keyval_rows[0]
    attended_seq, log_totals = attend_forward(query_seq, keyval_seq, length)
    attended_back = lax.all_to_all(
        attended_seq[None], "sp", split_axis=1, concat_axis=0, tiled=True
    )
    attended = join_groups(attended_back, row_count, seg_len, groups)
    proj = lax.psum(matmul(attended, output_weight).astype(jnp.bfloat16), "tp").astype(jnp.float32)
    resid = flat_inputs + proj + output_bias
    norm_two, hat_two, inv_two = normalize(resid, second_gain, second_bias)
    u_second = norm_two.astype(jnp.bfloat16)
    pre = matmul(u_second, up_weight) + up_bias
    hidden = gelu_tanh(pre).astype(jnp.bfloat16)
    mlp = lax.psum(matmul(hidden, down_weight).astype(jnp.bfloat16), "tp").astype(jnp.float32)
    outputs = (resid + mlp + down_bias).astype(jnp.bfloat16).reshape(row_count, seg_len, width)
    dout = cotangent.reshape(token_count, width).astype(jnp.float32)
    down_bias_grad = jnp.sum(dout, axis=0)
    dmlp = dout.astype(jnp.bfloat16)
    down_weight_grad = lead_product(hidden, dmlp)
    dhidden = tail_product(dmlp, down_weight)
    gelu_out, gelu_pull = jax.vjp(gelu_tanh, pre)
    dpre = gelu_pull(dhidden)[0].astype(jnp.bfloat16)
    up_bias_grad = jnp.sum(dpre.astype(jnp.float32), axis=0)
    up_weight_grad = lead_product(u_second, dpre)
    du_second = lax.psum(tail_product(dpre, up_weight).astype(jnp.bfloat16), "tp").astype(
        jnp.float32
    )
    dres_norm, second_gain_grad, second_bias_grad = norm_back(
        du_second, hat_two, inv_two, second_gain
    )
    dres = dout + dres_norm
    output_bias_grad = jnp.sum(dres, axis=0)
    dproj = dres.astype(jnp.bfloat16)
    output_weight_grad = lead_product(attended, dproj)
    dattended = tail_product(dproj, output_weight).astype(jnp.bfloat16)
    dattn_send = split_groups(dattended, row_count, seg_len, groups)
    dattn_seq = lax.all_to_all(dattn_send, "sp", split_axis=0, concat_axis=1, tiled=True)[0]
    dquery_seq, dkeyval_seq = attend_backward(query_seq, keyval_seq, length, log_totals, dattn_seq)
    dquery_back, dkeyval_back = (
        lax.all_to_all(
            dquery_seq.astype(jnp.float32)[None].astype(jnp.bfloat16),
            "sp",
            split_axis=1,
            concat_axis=0,
            tiled=True,
        ).astype(jnp.float32),
        lax.all_to_all(
            dkeyval_seq[None].astype(jnp.bfloat16), "sp", split_axis=1, concat_axis=0, tiled=True
        ).astype(jnp.float32),
    )
    dquery = join_groups(dquery_back, row_count, seg_len, groups).astype(jnp.bfloat16)
    dkeyval_part = jnp.sum(dkeyval_back.reshape(row_count, groups, seg_len, 2 * HD), axis=1)
    dkeyval_part = dkeyval_part.reshape(token_count, 2 * HD)
    dfirst_part, dkeyval_total = (
        lax.psum(tail_product(dquery, query_weight).astype(jnp.bfloat16), "tp").astype(jnp.float32),
        lax.psum(dkeyval_part.astype(jnp.bfloat16), "tp").astype(jnp.float32),
    )
    dkeyval = dkeyval_total.astype(jnp.bfloat16)
    dv_first = dfirst_part + tail_product(dkeyval, keyval_weight)
    query_weight_grad = lead_product(v_first, dquery)
    query_bias_grad = jnp.sum(dquery.astype(jnp.float32), axis=0)
    keyval_weight_grad = lead_product(v_first, dkeyval)
    value_bias_grad = jnp.sum(dkeyval[:, HD:].astype(jnp.float32), axis=0)
    dinput_norm, first_gain_grad, first_bias_grad = norm_back(
        dv_first, hat_one, inv_one, first_gain
    )
    input_grad = (dres + dinput_norm).astype(jnp.bfloat16).reshape(row_count, seg_len, width)
    part_sums = (
        lax.psum_scatter(
            query_weight_grad.astype(jnp.bfloat16), "dp", scatter_dimension=0, tiled=True
        ).astype(jnp.float32),
        lax.psum_scatter(
            keyval_weight_grad.astype(jnp.bfloat16), "dp", scatter_dimension=0, tiled=True
        ).astype(jnp.float32),
        lax.psum_scatter(
            output_weight_grad.astype(jnp.bfloat16), "dp", scatter_dimension=1, tiled=True
        ).astype(jnp.float32),
        lax.psum_scatter(
            up_weight_grad.astype(jnp.bfloat16), "dp", scatter_dimension=0, tiled=True
        ).astype(jnp.float32),
        lax.psum_scatter(
            down_weight_grad.astype(jnp.bfloat16), "dp", scatter_dimension=1, tiled=True
        ).astype(jnp.float32),
    )
    query_weight_grad, keyval_weight_grad, output_weight_grad, up_weight_grad, down_weight_grad = (
        lax.psum_scatter(
            part_sums[0].astype(jnp.bfloat16), "sp", scatter_dimension=0, tiled=True
        ).astype(jnp.float32),
        lax.psum_scatter(
            part_sums[1].astype(jnp.bfloat16), "sp", scatter_dimension=0, tiled=True
        ).astype(jnp.float32),
        lax.psum_scatter(
            part_sums[2].astype(jnp.bfloat16), "sp", scatter_dimension=1, tiled=True
        ).astype(jnp.float32),
        lax.psum_scatter(
            part_sums[3].astype(jnp.bfloat16), "sp", scatter_dimension=0, tiled=True
        ).astype(jnp.float32),
        lax.psum_scatter(
            part_sums[4].astype(jnp.bfloat16), "sp", scatter_dimension=1, tiled=True
        ).astype(jnp.float32),
    )
    small_total = lax.psum(
        (
            first_gain_grad,
            first_bias_grad,
            query_bias_grad,
            value_bias_grad,
            output_bias_grad,
            second_gain_grad,
            second_bias_grad,
            up_bias_grad,
            down_bias_grad,
        ),
        ("dp", "sp"),
    )
    return (
        outputs,
        input_grad,
        small_total[0],
        small_total[1],
        query_weight_grad,
        small_total[2],
        keyval_weight_grad,
        small_total[3],
        output_weight_grad,
        small_total[4],
        small_total[5],
        small_total[6],
        up_weight_grad,
        small_total[7],
        down_weight_grad,
        small_total[8],
    )


def solution(mesh):
    placed = (
        P("dp", "sp", None),
        P("dp"),
        P(),
        P(),
        P(None, "tp"),
        P("tp"),
        P(),
        P(),
        P("tp", None),
        P(),
        P(),
        P(),
        P(None, "tp"),
        P("tp"),
        P("tp", None),
        P(),
        P("dp", "sp", None),
    )
    return jax.shard_map(
        per_device,
        mesh=mesh,
        in_specs=placed,
        out_specs=(
            P("dp", "sp", None),
            P("dp", "sp", None),
            P(),
            P(),
            P(("dp", "sp"), "tp"),
            P("tp"),
            P(("dp", "sp"), None),
            P(),
            P("tp", ("dp", "sp")),
            P(),
            P(),
            P(),
            P(("dp", "sp"), "tp"),
            P("tp"),
            P("tp", ("dp", "sp")),
            P(),
        ),
        check_vma=False,
    )
```

profile of v0, /device:TPU:0, one launch (start us, length us, event | category | flops | bytes accessed | tf_op | source)
XLA Modules:
  0.0 1582.9 jit_solution(5752126598070808825)
XLA Ops:
  14.3 3.4 add_convert_fusion.2
  20.0 5.2 all-to-all-start.1
  31.7 7.8 all-to-all-done.1
  40.4 4.2 all-to-all-start
  48.6 9.5 all-to-all-done
  66.9 2.8 fusion.129
  75.0 3.3 fusion.130
  80.1 3.2 fusion.147
  86.6 3.5 fusion.131
  93.1 13.1 copy.288
  106.7 12.6 reduce.23
  119.3 3.5 reshape.731
  122.8 17.9 %all_to_all.60 = bf16[4,2,65536]{2,1,0:T(2,128)(2,1)} all-to-all(bf16[4,2,65536]{2,1,0:T(2,128)(2,1)} %reshape.731), channel_id=1, replica_groups=mesh['dp'=4,'sp'=4,'tp'=2] {'sp'}, dimensions={0} | all-to-all | bytes 2097152 | tf_op jit(solution)/shard_map/all_to_all | solution.py:184
  140.7 4.0 reshape.732
  149.7 6.2 convolution_convert_fusion.5
  156.0 21.0 %all-reduce.10.cloned.1.call-done = bf16[512,2048]{1,0:T(8,128)(2,1)} async-done(((bf16[512,2048]{1,0:T(8,128)(2,1)}), bf16[512,2048]{1,0:T(8,128)(2,1)}) %all-reduce.10.cloned.1.call-update) | async-done | bytes 2097168 | tf_op jit(solution)/shard_map/psum | solution.py:188
  180.6 15.3 fusion.143
  195.9 21.0 %convert_reduce_fusion = (f32[4096]{0:T(1024)}, bf16[512,4096]{1,0:T(8,128)(2,1)}) fusion(f32[512,4096]{1,0:T(8,128)} %fusion.143, f32[4096]{0:T(1024)S(1)} %copy-done.41, bf16[4096,2048]{1,0:T(8,128)(2,1)} %param.51, bf16[1,512,2048]{2,1,0:T(8,128)(2,1)} %param.53), kind=kOutput, calls=%fused_computation.17 | convolution fusion | flops 8638164992 | bytes 31490048 | tf_op jit(solution)/shard_map/dot_general | solution.py:27
  216.9 14.8 convolution_convert_fusion.6
  231.7 22.5 %all-reduce.12.cloned.1.call-done = bf16[512,2048]{1,0:T(8,128)(2,1)} async-done(((bf16[512,2048]{1,0:T(8,128)(2,1)}), bf16[512,2048]{1,0:T(8,128)(2,1)}) %all-reduce.12.cloned.1.call-update) | async-done | bytes 2097168 | tf_op jit(solution)/shard_map/psum | solution.py:205
  254.2 5.0 fusion.45
  259.3 3.9 fusion.144
  265.3 3.4 convolution_convert_fusion.9
  270.9 4.5 all-to-all-start.3
  275.4 14.4 all-to-all-done.3
  298.7 3.8 fusion.48
  303.4 4.8 fusion.12
  313.6 4.6 fusion.50
  324.2 6.4 fusion.14
  337.6 5.4 fusion.7
  352.9 12.7 fusion.151
  365.6 12.6 reduce.24
  378.2 3.5 reshape.733
  381.7 4.2 all-to-all-start.4
  385.9 5.2 fusion.86
  392.3 5.9 copy.234
  398.2 12.6 reduce.25
  410.8 3.4 reshape.735
  414.2 4.2 all-to-all-start.5
  418.5 17.8 %convolution_convert_fusion.7 = bf16[512,2048]{1,0:T(8,128)(2,1)} fusion(bf16[4096,2048]{1,0:T(8,128)(2,1)} %param.51, f32[512,4096]{1,0:T(8,128)} %fusion.143, f32[4096]{0:T(1024)S(1)} %copy-done.41), kind=kOutput, calls=%fused_computation.104 | convolution fusion | flops 8611954688 | bytes 27279360 | tf_op jit(solution)/shard_map/dot_general | solution.py:17
  436.4 4.0 reshape.734
  445.3 4.0 reshape.736
  449.3 2.7 copy.284
  454.3 6.2 convolution_convert_fusion.4
  460.6 30.8 %all-reduce.16.cloned.1.call-done = (bf16[512,2048]{1,0:T(8,128)(2,1)}, bf16[512,2048]{1,0:T(8,128)(2,1)}, bf16[512,256]{0,1:T(8,128)(2,1)}) async-done(((bf16[512,2048]{1,0:T(8,128)(2,1)}, bf16[512,2048]{1,0:T(8,128)(2,1)}, bf16[512,256]{0,1:T(8,128)(2,1)}), (bf16[512,2048]{1,0:T(8,128)(2,1)}, bf16[512,2048]{1,0:T(8,128)(2,1)}, bf16[512,256]{0,1:T(8,128)(2,1)})) %all-reduce.16.cloned.1.call-update) | async-done | bytes 4456464 | tf_op jit(solution)/shard_map/psum | solution.py:194
  491.4 3.3 convolution_convert_fusion.8
  494.8 6.8 convolution_convert_fusion.2
  502.4 5.8 convolution_convert_fusion.3
  508.2 17.1 %convolution_convert_fusion = bf16[4096,2048]{1,0:T(8,128)(2,1)} fusion(bf16[1,512,2048]{2,1,0:T(8,128)(2,1)} %param.53, f32[512,4096]{1,0:T(8,128)} %fusion.143, f32[4096]{0:T(1024)S(1)} %copy-done.41), kind=kOutput, calls=%fused_computation | convolution fusion | flops 8619294720 | bytes 27279360 | tf_op jit(solution)/shard_map/dot_general | solution.py:21
  526.0 15.3 convolution_convert_fusion.1
  542.1 58.8 %reduce-scatter.23.cloned.1.call-done = bf16[1024,512]{1,0:T(8,128)(2,1)} async-done(((bf16[1024,2048]{1,0:T(8,128)(2,1)}), bf16[1024,512]{1,0:T(8,128)(2,1)}) %reduce-scatter.23.cloned.1.call-update) | async-done | bytes 1048592 | tf_op jit(solution)/shard_map/reduce_scatter | solution.py:255
  603.2 77.2 %reduce-scatter.15.cloned.1.call-done = bf16[512,1024]{1,0:T(8,128)(2,1)} async-done(((bf16[2048,1024]{1,0:T(8,128)(2,1)}), bf16[512,1024]{1,0:T(8,128)(2,1)}) %reduce-scatter.15.cloned.1.call-update) | async-done | bytes 1048592 | tf_op jit(solution)/shard_map/reduce_scatter | solution.py:249
  680.5 283.1 %reduce-scatter.29.cloned.1.call-done = bf16[4096,512]{1,0:T(8,128)(2,1)} async-done(((bf16[4096,2048]{1,0:T(8,128)(2,1)}), bf16[4096,512]{1,0:T(8,128)(2,1)}) %reduce-scatter.29.cloned.1.call-update) | async-done | bytes 4194320 | tf_op jit(solution)/shard_map/reduce_scatter | solution.py:261
  963.6 6.4 copy.280
  970.1 277.1 %reduce-scatter.25.cloned.1.call-done = bf16[512,4096]{1,0:T(8,128)(2,1)} async-done(((bf16[2048,4096]{1,0:T(8,128)(2,1)}), bf16[512,4096]{1,0:T(8,128)(2,1)}) %reduce-scatter.25.cloned.1.call-update) | async-done | bytes 4194320 | tf_op jit(solution)/shard_map/reduce_scatter | solution.py:258
  1249.8 5.5 fusion.35
  1255.4 7.4 fusion.94
  1262.8 11.9 reduce-scatter.21.cloned.1.call-done
  1276.2 29.8 %reduce-scatter.31.cloned.1.call-done = bf16[128,1024]{1,0:T(8,128)(2,1)} async-done(((bf16[512,1024]{1,0:T(8,128)(2,1)}), bf16[128,1024]{1,0:T(8,128)(2,1)}) %reduce-scatter.31.cloned.1.call-update) | async-done | bytes 262160
  1308.0 28.7 %reduce-scatter.17.cloned.1.call-done = bf16[128,1024]{1,0:T(8,128)(2,1)} async-done(((bf16[512,1024]{1,0:T(8,128)(2,1)}), bf16[128,1024]{1,0:T(8,128)(2,1)}) %reduce-scatter.17.cloned.1.call-update) | async-done | bytes 262160 | tf_op jit(solution)/shard_map/reduce_scatter | solution.py:266
  1338.5 54.0 %reduce-scatter.33.cloned.1.call-done = bf16[128,4096]{1,0:T(8,128)(2,1)} async-done(((bf16[512,4096]{1,0:T(8,128)(2,1)}), bf16[128,4096]{1,0:T(8,128)(2,1)}) %reduce-scatter.33.cloned.1.call-update) | async-done | bytes 1048592
  1395.6 52.6 %reduce-scatter.27.cloned.1.call-done = bf16[128,4096]{1,0:T(8,128)(2,1)} async-done(((bf16[512,4096]{1,0:T(8,128)(2,1)}), bf16[128,4096]{1,0:T(8,128)(2,1)}) %reduce-scatter.27.cloned.1.call-update) | async-done | bytes 1048592 | tf_op jit(solution)/shard_map/reduce_scatter | solution.py:275
  1448.2 2.8 convert_element_type.309
  1451.0 113.7 %all-reduce.14.cloned.1.call-done = (f32[2048]{0:T(1024)}, f32[2048]{0:T(1024)}, f32[1024]{0:T(1024)}, f32[128]{0:T(128)}, f32[2048]{0:T(1024)}, /*index=5*/f32[...) async-done(((f32[2048]{0:T(1024)}, f32[2048]{0:T(1024)}, f32[1024]{0:T(1024)}, f32[128]{0:T(128)}, f32[2048]{0:T(1024)}, /*index=5*/f32[2048]{0:T(1024)}, ...) | async-done | bytes 70160 | tf_op jit(solution)/shard_map/psum | solution.py:282
  (225 shorter events, 129.3 us)
Async XLA Ops:
  7.2 20.7 %copy-start = (bf16[2048,256]{1,0:T(8,128)(2,1)S(1)}, bf16[2048,256]{1,0:T(8,128)(2,1)}, u32[]{:S(2)}) copy-start(bf16[2048,256]{1,0:T(8,128)(2,1)} %param.43) | copy-start | bytes 3145732
  7.2 4.9 copy-start.2
  7.2 4.9 copy-start.30
  7.2 4.9 copy-start.35
  7.2 7.1 copy-start.40
  7.2 7.1 copy-start.44
  9.4 2.7 copy-start.28
  12.1 0.9 copy-start.33
  13.0 1.3 copy-start.17
  17.7 10.2 copy-start.38
  20.0 19.4 %all-to-all-start.1 = ((bf16[4,512,256]{1,2,0:T(8,128)(2,1)}), bf16[4,512,256]{1,2,0:T(8,128)(2,1)}, u32[]{:S(2)}, u32[]{:S(2)}) async-start(bf16[4,512,256]{1,2,0:T(8,128)(2,1)} %bitcast.366), calls=%async_computation.1 | async-start | bytes 2097152 | tf_op jit(solution)/shard_map/all_to_all | solution.py:178
  40.4 17.7 %all-to-all-start = ((bf16[4,512,256]{2,1,0:T(8,128)(2,1)}), bf16[4,512,256]{2,1,0:T(8,128)(2,1)}, u32[]{:S(2)}, u32[]{:S(2)}) async-start(bf16[4,512,256]{2,1,0:T(8,128)(2,1)} %reshape.682), calls=%async_computation | async-start | bytes 2097152 | tf_op jit(solution)/shard_map/all_to_all | solution.py:179
  44.7 132.3 %all-reduce.10.cloned.1.call-start = ((), (), s32[]{:S(2)}) async-start(), calls=%async_computation.16 | async-start | bytes 4194304 | tf_op jit(solution)/shard_map/psum | solution.py:188
  48.6 31.5 %copy-start.20 = (bf16[1,512,256]{1,2,0:T(8,128)(2,1)}, bf16[1,512,256]{1,2,0:T(8,128)(2,1)S(1)}, u32[]{:S(2)}) copy-start(bf16[1,512,256]{1,2,0:T(8,128)(2,1)S(1)} %get-tuple-element.158) | copy-start | bytes 786436
  59.7 2.6 copy-start.8
  66.3 3.4 copy-start.4
  74.2 4.2 copy-start.3
  83.3 3.3 copy-start.1
  86.6 5.3 copy-start.23
  149.7 27.3 %copy-start.26 = (f32[2048]{0:T(1024)S(1)}, f32[2048]{0:T(1024)}, u32[]{:S(2)}) copy-start(f32[2048]{0:T(1024)} %param.46) | copy-start | bytes 24580
  155.9 24.7 %copy-start.32 = (f32[2048]{0:T(1024)S(1)}, f32[2048]{0:T(1024)}, u32[]{:S(2)}) copy-start(f32[2048]{0:T(1024)} %param.47) | copy-start | bytes 24580
  155.9 24.7 %copy-start.42 = (f32[2048]{0:T(1024)S(1)}, f32[2048]{0:T(1024)}, u32[]{:S(2)}) copy-start(f32[2048]{0:T(1024)} %param.48) | copy-start | bytes 24580
  155.9 98.3 %all-reduce.12.cloned.1.call-start = ((), (), s32[]{:S(2)}) async-start(), calls=%async_computation.17 | async-start | bytes 4194304 | tf_op jit(solution)/shard_map/psum | solution.py:205
  177.0 2.5 copy-start.6
  180.6 15.3 copy-start.41
  254.2 5.1 copy-start.7
  254.2 5.1 copy-start.16
  254.2 5.1 copy-start.18
  259.3 6.0 copy-start.39
  263.2 2.0 copy-start.15
  270.9 18.9 %all-to-all-start.3 = ((bf16[4,512,256]{1,2,0:T(8,128)(2,1)}), bf16[4,512,256]{1,2,0:T(8,128)(2,1)}, u32[]{:S(2)}, u32[]{:S(2)}) async-start(bf16[4,512,256]{1,2,0:T(8,128)(2,1)} %bitcast.367), calls=%async_computation.3 | async-start | bytes 2097152 | tf_op jit(solution)/shard_map/all_to_all | solution.py:217
  289.8 3.5 copy-start.9
  293.4 2.0 copy-start.24
  294.8 3.9 copy-start.5
  298.6 4.8 slice-start.2
  298.7 4.7 slice-start.3
  309.6 1.0 copy-start.10
  313.6 6.8 copy-start.25
  321.3 1.0 copy-start.11
  324.2 8.8 copy-start.22
  330.5 2.4 copy-start.12
  334.2 1.0 copy-start.13
  337.6 5.4 slice-start
  337.6 6.0 slice-start.1
  346.0 2.6 copy-start.14
  346.0 2.6 copy-start.21
  381.7 32.6 %all-to-all-start.4 = ((bf16[4,2,65536]{2,1,0:T(2,128)(2,1)}), bf16[4,2,65536]{2,1,0:T(2,128)(2,1)}, u32[]{:S(2)}, u32[]{:S(2)}) async-start(bf16[4,2,65536]{2,1,0:T(2,128)(2,1)} %reshape.733), calls=%async_computation.4 | async-start | bytes 2097152 | tf_op jit(solution)/shard_map/all_to_all | solution.py:220
  385.9 5.3 copy-start.19
  414.2 31.1 %all-to-all-start.5 = ((bf16[4,2,65536]{2,1,0:T(2,128)(2,1)}), bf16[4,2,65536]{2,1,0:T(2,128)(2,1)}, u32[]{:S(2)}, u32[]{:S(2)}) async-start(bf16[4,2,65536]{2,1,0:T(2,128)(2,1)} %reshape.735), calls=%async_computation.5 | async-start | bytes 2097152 | tf_op jit(solution)/shard_map/all_to_all | solution.py:227
  418.5 72.9 %all-reduce.16.cloned.1.call-start = ((), (), s32[]{:S(2)}) async-start(), calls=%async_computation.29 | async-start | bytes 8912896 | tf_op jit(solution)/shard_map/psum | solution.py:194
  460.6 80.8 %reduce-scatter.19.cloned.1.call-start = ((), (), s32[]{:S(2)}) async-start(), calls=%async_computation.20 | async-start | bytes 1310720 | tf_op jit(solution)/shard_map/reduce_scatter | solution.py:252
  494.8 106.1 %reduce-scatter.23.cloned.1.call-start = ((), (), s32[]{:S(2)}) async-start(), calls=%async_computation.22 | async-start | bytes 5242880 | tf_op jit(solution)/shard_map/reduce_scatter | solution.py:255
  501.6 0.7 copy-start.36
  501.7 178.7 %reduce-scatter.15.cloned.1.call-start = ((), (), s32[]{:S(2)}) async-start(), calls=%async_computation.18 | async-start | bytes 5242880 | tf_op jit(solution)/shard_map/reduce_scatter | solution.py:249
  508.2 455.4 %reduce-scatter.29.cloned.1.call-start = ((), (), s32[]{:S(2)}) async-start(), calls=%async_computation.25 | async-start | bytes 20971520 | tf_op jit(solution)/shard_map/reduce_scatter | solution.py:261
  525.3 721.8 %reduce-scatter.25.cloned.1.call-start = ((), (), s32[]{:S(2)}) async-start(), calls=%async_computation.23 | async-start | bytes 20971520 | tf_op jit(solution)/shard_map/reduce_scatter | solution.py:258
  541.3 733.5 %reduce-scatter.21.cloned.1.call-start = ((), (), s32[]{:S(2)}) async-start(), calls=%async_computation.21 | async-start | bytes 327680 | tf_op jit(solution)/shard_map/reduce_scatter | solution.py:269
  542.0 764.0 %reduce-scatter.31.cloned.1.call-start = ((), (), s32[]{:S(2)}) async-start(), calls=%async_computation.26 | async-start | bytes 1310720
  603.1 733.6 %reduce-scatter.17.cloned.1.call-start = ((), (), s32[]{:S(2)}) async-start(), calls=%async_computation.19 | async-start | bytes 1310720 | tf_op jit(solution)/shard_map/reduce_scatter | solution.py:266
  680.4 712.2 %reduce-scatter.33.cloned.1.call-start = ((), (), s32[]{:S(2)}) async-start(), calls=%async_computation.27 | async-start | bytes 5242880
  970.0 279.2 %copy-start.27 = (bf16[512,256]{0,1:T(8,128)(2,1)S(1)}, bf16[512,256]{0,1:T(8,128)(2,1)}, u32[]{:S(2)}) copy-start(bf16[512,256]{0,1:T(8,128)(2,1)} %get-tuple-element.147) | copy-start | bytes 786436
  970.0 478.2 %reduce-scatter.27.cloned.1.call-start = ((), (), s32[]{:S(2)}) async-start(), calls=%async_computation.24 | async-start | bytes 5242880 | tf_op jit(solution)/shard_map/reduce_scatter | solution.py:275
  1247.1 317.5 %all-reduce.14.cloned.1.call-start = ((), (), s32[]{:S(2)}) async-start(), calls=%async_computation.28 | async-start | bytes 140288 | tf_op jit(solution)/shard_map/psum | solution.py:282
  1249.8 5.6 copy-start.37
  (4 other events, 2.8 us)
Sparse Core Ops, SparseCore 0:
  156.0 20.9 all-reduce.9
  231.8 22.3 all-reduce.11
  460.7 30.6 all-reduce.15
  494.9 28.2 reduce-scatter.18
  525.4 75.4 reduce-scatter.22
  603.1 77.2 reduce-scatter.14
  682.7 280.7 reduce-scatter.28
  966.1 281.0 reduce-scatter.24
  1249.9 24.8 reduce-scatter.20
  1278.3 27.7 reduce-scatter.30
  1309.0 27.7 reduce-scatter.16
  1339.8 52.6 reduce-scatter.32
  1395.5 52.6 reduce-scatter.26
  1456.8 107.8 all-reduce.13
where the time goes:
time: 1590 us; the launch traced here: 1580 us
  waiting for transfers between devices  1090 us (69%)
  matrix products  205 us (13%)
  local copies, waits for them, and re-layouts  115 us (7%)
  other arithmetic  112 us (7%)
  starting transfers between devices  23.4 us (1%)
  blocking collectives  17.9 us (1%)
    reduce_scatter x1, waiting for transfers between devices, per_device(): lax.psum_scatter(down_weight_grad.astype(jnp.bfloat16), 'dp', scatter_dim...  283 us
    reduce_scatter x1, waiting for transfers between devices, per_device(): lax.psum_scatter(up_weight_grad.astype(jnp.bfloat16), 'dp', scatter_dimen...  277 us
    psum x1, waiting for transfers between devices, per_device(): lax.psum((first_gain_grad, first_bias_grad, query_bias_grad, value_bias_g...  114 us
    unnamed x16, waiting for transfers between devices  84.7 us
    reduce_scatter x1, waiting for transfers between devices, per_device(): lax.psum_scatter(query_weight_grad.astype(jnp.bfloat16), 'dp', scatter_di...  77.2 us
    unnamed x123, local copies, waits for them, and re-layouts  65.3 us
    reduce_scatter x1, waiting for transfers between devices, per_device(): lax.psum_scatter(output_weight_grad.astype(jnp.bfloat16), 'dp', scatter_d...  58.8 us
    reduce_scatter x1, waiting for transfers between devices, per_device(): lax.psum_scatter(part_sums[3].astype(jnp.bfloat16), 'sp', scatter_dimensi...  52.6 us
  transfers between devices with their start and end apart: 19, of which 16 were waited for; matrix products, arithmetic and copies ran while one was open for 9% of the time, Pallas kernels for 0%

commit v1 on v0

v1 whole, which is shorter than its diff:
```python
import functools
import math

import jax
import jax.numpy as jnp
from jax import lax
from jax.experimental import pallas as pl
from jax.experimental.pallas import tpu as pltpu
from jax.sharding import PartitionSpec as P

HD = 128
EPS = 1e-05
BF = jnp.bfloat16
F32 = jnp.float32
SCALE = 1.0 / math.sqrt(HD)
SCALE2 = SCALE * math.log2(math.e)
VMEM = 60 * 2**20
GELU_A = math.sqrt(2.0 / math.pi)
GELU_B = 0.044715


def nn(left, right):
    return jnp.dot(left, right, preferred_element_type=F32)


def nt(left, right):
    return lax.dot_general(left, right, (((1,), (1,)), ((), ())), preferred_element_type=F32)


def tn(left, right):
    return lax.dot_general(left, right, (((0,), (0,)), ((), ())), preferred_element_type=F32)


def params():
    return pltpu.CompilerParams(vmem_limit_bytes=VMEM)


def chunk_mask(first, length, chunk, size, seg, wide):
    key_pos = chunk * size + lax.broadcasted_iota(jnp.int32, (size, wide), 0)
    query_pos = first + lax.rem(lax.broadcasted_iota(jnp.int32, (size, wide), 1), seg)
    return (key_pos <= query_pos) & (key_pos < length)


def chunk_bounds(info_ref, row, seg, size):
    first, length = info_ref[0], info_ref[1 + row]
    full = jnp.minimum(first + 1, length) // size
    total = (jnp.minimum(first + seg, length) + size - 1) // size
    return first, length, full, total


def stack_heads(ref, heads):
    return jnp.concatenate([ref[0, :, h * HD : (h + 1) * HD] for h in range(heads)], axis=0)


def unstack_heads(ref, values, heads, seg):
    for h in range(heads):
        ref[0, :, h * HD : (h + 1) * HD] = values[h * seg : (h + 1) * seg]


def forward_kernel(size, heads, seg, info_ref, q_ref, k_ref, vt_ref, o_ref, lse_ref, top_s, sum_s, acc_s):
    first, length, full, total = chunk_bounds(info_ref, pl.program_id(0), seg, size)
    q = stack_heads(q_ref, heads)
    top_s[...] = jnp.full_like(top_s, -1e30)
    sum_s[...] = jnp.zeros_like(sum_s)
    acc_s[...] = jnp.zeros_like(acc_s)

    def step(masked, chunk, carry):
        at = pl.multiple_of(chunk * size, size)
        scores = nt(k_ref[0, pl.ds(at, size), :], q) * SCALE2
        if masked:
            scores = jnp.where(chunk_mask(first, length, chunk, size, seg, heads * seg), scores, -1e30)
        old = top_s[...]
        new = jnp.maximum(old, jnp.max(scores, axis=0, keepdims=True))
        weights = jnp.exp2(scores - new)
        shrink = jnp.exp2(old - new)
        sum_s[...] = sum_s[...] * shrink + jnp.sum(weights, axis=0, keepdims=True)
        acc_s[...] = acc_s[...] * shrink + nn(vt_ref[0, :, pl.ds(at, size)], weights.astype(BF))
        top_s[...] = new
        return carry

    lax.fori_loop(0, full, functools.partial(step, False), 0)
    lax.fori_loop(full, total, functools.partial(step, True), 0)
    unstack_heads(o_ref, (acc_s[...] * (1.0 / sum_s[...])).T.astype(BF), heads, seg)
    lse_ref[0, 0] = top_s[...] + jnp.log2(sum_s[...])


def attend_forward(info, query, keys, values_t, size, heads):
    rows, seg, width = query.shape
    length = keys.shape[1]
    groups, wide = width // (HD * heads), heads * seg
    head_spec = pl.BlockSpec((1, seg, heads * HD), lambda r, h, info: (r, 0, h))
    return pl.pallas_call(
        functools.partial(forward_kernel, size, heads, seg),
        grid_spec=pltpu.PrefetchScalarGridSpec(
            num_scalar_prefetch=1,
            grid=(rows, groups),
            in_specs=[
                head_spec,
                pl.BlockSpec((1, length, HD), lambda r, h, info: (r, 0, 0)),
                pl.BlockSpec((1, HD, length), lambda r, h, info: (r, 0, 0)),
            ],
            out_specs=[head_spec, pl.BlockSpec((1, 1, 1, wide), lambda r, h, info: (r, h, 0, 0))],
            scratch_shapes=[pltpu.VMEM((1, wide), F32), pltpu.VMEM((1, wide), F32), pltpu.VMEM((HD, wide), F32)],
        ),
        out_shape=[
            jax.ShapeDtypeStruct((rows, seg, width), BF),
            jax.ShapeDtypeStruct((rows, groups, 1, wide), F32),
        ],
        compiler_params=params(),
        cost_estimate=pl.CostEstimate(flops=8 * 10**9, bytes_accessed=4 * 2**20, transcendentals=8 * 10**6),
        name="attend_forward",
    )(info, query, keys, values_t)


def backward_kernel(
    size, heads, seg, info_ref, q_ref, do_ref, o_ref, lse_ref, k_ref, v_ref, kt_ref, dq_ref, dkv_ref, dqt_s
):
    first, length, full, total = chunk_bounds(info_ref, pl.program_id(0), seg, size)

    @pl.when(pl.program_id(1) == 0)
    def _():
        dkv_ref[...] = jnp.zeros_like(dkv_ref)

    q, dout, out = (stack_heads(ref, heads) for ref in (q_ref, do_ref, o_ref))
    delta = jnp.sum((dout.astype(F32) * out.astype(F32)).T, axis=0, keepdims=True)
    lse = lse_ref[0, 0]
    dqt_s[...] = jnp.zeros_like(dqt_s)

    def step(masked, chunk, carry):
        at = pl.multiple_of(chunk * size, size)
        prob = jnp.exp2(nt(k_ref[0, pl.ds(at, size), :], q) * SCALE2 - lse)
        if masked:
            prob = jnp.where(chunk_mask(first, length, chunk, size, seg, heads * seg), prob, 0.0)
        dprob = nt(v_ref[0, pl.ds(at, size), :], dout)
        dscore = (prob * (dprob - delta)).astype(BF)
        dkv_ref[0, pl.ds(at, size), HD:] += nn(prob.astype(BF), dout)
        dkv_ref[0, pl.ds(at, size), :HD] += nn(dscore, q) * SCALE
        dqt_s[...] += nn(kt_ref[0, :, pl.ds(at, size)], dscore)
        return carry

    lax.fori_loop(0, full, functools.partial(step, False), 0)
    lax.fori_loop(full, total, functools.partial(step, True), 0)
    unstack_heads(dq_ref, (dqt_s[...] * SCALE).T.astype(BF), heads, seg)


def attend_backward(info, query, dout, out, lse, keys, values, keys_t, size, heads):
    rows, seg, width = query.shape
    length = keys.shape[1]
    groups, wide = width // (HD * heads), heads * seg
    head_spec = pl.BlockSpec((1, seg, heads * HD), lambda r, h, info: (r, 0, h))
    key_spec = pl.BlockSpec((1, length, HD), lambda r, h, info: (r, 0, 0))
    return pl.pallas_call(
        functools.partial(backward_kernel, size, heads, seg),
        grid_spec=pltpu.PrefetchScalarGridSpec(
            num_scalar_prefetch=1,
            grid=(rows, groups),
            in_specs=[
                head_spec,
                head_spec,
                head_spec,
                pl.BlockSpec((1, 1, 1, wide), lambda r, h, info: (r, h, 0, 0)),
                key_spec,
                key_spec,
                pl.BlockSpec((1, HD, length), lambda r, h, info: (r, 0, 0)),
            ],
            out_specs=[head_spec, pl.BlockSpec((1, length, 2 * HD), lambda r, h, info: (r, 0, 0))],
            scratch_shapes=[pltpu.VMEM((HD, wide), F32)],
        ),
        out_shape=[
            jax.ShapeDtypeStruct((rows, seg, width), BF),
            jax.ShapeDtypeStruct((rows, length, 2 * HD), F32),
        ],
        compiler_params=params(),
        cost_estimate=pl.CostEstimate(flops=16 * 10**9, bytes_accessed=8 * 2**20, transcendentals=8 * 10**6),
        name="attend_backward",
    )(info, query, dout, out, lse, keys, values, keys_t)


def gelu_parts(v):
    square = v * v
    t = jnp.tanh(GELU_A * v * (1.0 + GELU_B * square))
    half = 0.5 * (1.0 + t)
    slope = half + 0.5 * v * (1.0 - t * t) * (GELU_A * (1.0 + 3.0 * GELU_B * square))
    return v * half, slope


def local_kernel(u_ref, dm_ref, up_ref, down_ref, bias_ref, mlp_ref, du_ref, dbias_ref, mlp_s, du_s):
    step = pl.program_id(0)

    @pl.when(step == 0)
    def _():
        mlp_s[...] = jnp.zeros_like(mlp_s)
        du_s[...] = jnp.zeros_like(du_s)

    hidden, slope = gelu_parts(nn(u_ref[...], up_ref[...]) + bias_ref[...])
    mlp_s[...] += nn(hidden.astype(BF), down_ref[...])
    dpre = (nt(dm_ref[...], down_ref[...]) * slope).astype(BF)
    dbias_ref[...] = jnp.sum(dpre.astype(F32), axis=0, keepdims=True)
    du_s[...] += nt(dpre, up_ref[...])

    @pl.when(step == pl.num_programs(0) - 1)
    def _():
        mlp_ref[...] = mlp_s[...].astype(BF)
        du_ref[...] = du_s[...].astype(BF)


def feed_local(u, dmlp, up, down, bias, tile):
    tokens, width = u.shape
    units = up.shape[1]
    whole = pl.BlockSpec((tokens, width), lambda i: (0, 0))
    return pl.pallas_call(
        local_kernel,
        grid=(units // tile,),
        in_specs=[
            whole,
            whole,
            pl.BlockSpec((width, tile), lambda i: (0, i)),
            pl.BlockSpec((tile, width), lambda i: (i, 0)),
            pl.BlockSpec((1, tile), lambda i: (0, i)),
        ],
        out_specs=[whole, whole, pl.BlockSpec((1, tile), lambda i: (0, i))],
        out_shape=[
            jax.ShapeDtypeStruct((tokens, width), BF),
            jax.ShapeDtypeStruct((tokens, width), BF),
            jax.ShapeDtypeStruct((1, units), F32),
        ],
        scratch_shapes=[pltpu.VMEM((tokens, width), F32)] * 2,
        compiler_params=params(),
        cost_estimate=pl.CostEstimate(
            flops=8 * tokens * width * units, bytes_accessed=4 * width * units, transcendentals=tokens * units
        ),
        name="feed_local",
    )(u, dmlp, up, down, bias)


def grad_kernel(at_ref, u_ref, dm_ref, up_ref, down_ref, bias_ref, out_ref):
    tile = up_ref.shape[1]
    hidden, slope = gelu_parts(nn(u_ref[...], up_ref[...]) + bias_ref[...])
    dpre = (nt(dm_ref[...], down_ref[...]) * slope).astype(BF)
    out_ref[:, :tile] = tn(u_ref[...], dpre).astype(BF)
    out_ref[:, tile:] = tn(dm_ref[...], hidden.astype(BF)).astype(BF)


def feed_grads(at, u, dmlp, up, down, bias, tile, count):
    tokens, width = u.shape
    whole = pl.BlockSpec((tokens, width), lambda i, at: (0, 0), pipeline_mode=pl.Buffered(1))
    return pl.pallas_call(
        grad_kernel,
        grid_spec=pltpu.PrefetchScalarGridSpec(
            num_scalar_prefetch=1,
            grid=(count,),
            in_specs=[
                whole,
                whole,
                pl.BlockSpec((width, tile), lambda i, at: (0, at[0] + i)),
                pl.BlockSpec((tile, width), lambda i, at: (at[0] + i, 0)),
                pl.BlockSpec((1, tile), lambda i, at: (0, at[0] + i)),
            ],
            out_specs=pl.BlockSpec((width, 2 * tile), lambda i, at: (0, i)),
        ),
        out_shape=jax.ShapeDtypeStruct((width, 2 * tile * count), BF),
        compiler_params=params(),
        cost_estimate=pl.CostEstimate(
            flops=8 * tokens * width * tile * count, bytes_accessed=4 * width * (tokens + 2 * tile * count), transcendentals=0
        ),
        name="feed_grads",
    )(at, u, dmlp, up, down, bias)


def normalize(values):
    average = jnp.mean(values, axis=-1, keepdims=True)
    centered = values - average
    variance = jnp.mean(centered * centered, axis=-1, keepdims=True)
    inv_std = lax.rsqrt(variance + EPS)
    return centered * inv_std, inv_std


def norm_back(gradient, scaled, inv_std, norm_gain):
    inner = gradient * norm_gain
    mean_one = jnp.mean(inner, axis=-1, keepdims=True)
    mean_two = jnp.mean(inner * scaled, axis=-1, keepdims=True)
    back = inv_std * (inner - mean_one - scaled * mean_two)
    return back, jnp.sum(gradient * scaled, axis=0), jnp.sum(gradient, axis=0)


def build(mesh):
    sp_size, dp_size = mesh.shape["sp"], mesh.shape["dp"]
    quads = sp_size // 4

    def swap(value, bit):
        return lax.ppermute(value, "sp", [(i, i ^ bit) for i in range(sp_size)])

    def swap_dp(value, bit):
        return lax.ppermute(value, "dp", [(i, i ^ bit) for i in range(dp_size)])

    def swap_tp(value):
        return lax.ppermute(value, "tp", [(0, 1), (1, 0)])

    def tp_sum(part):
        part = lax.optimization_barrier(part)
        other = swap_tp(part)
        return part.astype(F32) + other.astype(F32)

    def sum_all(vector):
        for bit in (1 << k for k in range(sp_size.bit_length() - 1)):
            vector = vector + swap(vector, bit)
        for bit in (1 << k for k in range(dp_size.bit_length() - 1)):
            vector = vector + swap_dp(vector, bit)
        return vector

    def gather_quad(own, core):
        half = own.shape[0] // 2
        mine = lax.dynamic_slice_in_dim(own, core * half, half, 0)
        from_x, from_y = swap(mine, 1), swap(mine, 2)
        far = (swap(from_x[: half // 2], 2), swap(from_y[half // 2 :], 1))
        parts = [from_x, from_y, *far]
        return jnp.concatenate([own, *parts, *[swap_tp(part) for part in parts]], axis=0)

    def scatter_quad(blocks):
        blocks = [block.astype(BF) for block in blocks]
        half = blocks[0].shape[0] // 2
        low, high = [b[:half] for b in blocks], [b[half:] for b in blocks]
        low_one, low_pass = swap(low[1], 1), swap(low[3], 1)
        high_one, high_pass = swap(high[2], 2), swap(high[3], 2)
        add = lambda *terms: sum(t.astype(F32) for t in terms)
        low_two = swap(add(low[2], low_pass).astype(BF), 2)
        high_two = swap(add(high[1], high_pass).astype(BF), 1)
        return jnp.concatenate([add(low[0], low_one, low_two), add(high[0], high_one, high_two)], axis=0).astype(BF)

    def scatter_rest(value):
        lead = value.shape[2]
        columns = value.shape[3]
        value = lax.psum_scatter(value.reshape(-1, columns), "dp", scatter_dimension=0, tiled=True)
        if quads > 1:
            groups = [[q * 4 + r for q in range(quads)] for r in range(4)]
            value = lax.psum_scatter(value, "sp", scatter_dimension=0, tiled=True, axis_index_groups=groups)
        return value.reshape(lead, columns)

    def per_device(
        inputs, lengths, first_gain, first_bias, query_weight, query_bias, keyval_weight, value_bias, output_weight,
        output_bias, second_gain, second_bias, up_weight, up_bias, down_weight, down_bias, cotangent,
    ):
        rows, seg, width = inputs.shape
        tokens = rows * seg
        place, core = lax.axis_index("sp"), lax.axis_index("tp")
        spot = lax.rem(place, 4)
        row_len = seg * sp_size
        info = jnp.concatenate([(place * seg).astype(jnp.int32).reshape(1), lengths])
        shard = width // (dp_size * sp_size)

        x = inputs.reshape(tokens, width).astype(F32)
        dmlp = cotangent.reshape(tokens, width)
        hat_one, inv_one = normalize(x)
        v_first = (hat_one * first_gain + first_bias).astype(BF)
        kv_bias = jnp.concatenate([jnp.zeros((HD,), F32), value_bias])
        keyval = (nn(v_first, keyval_weight) + kv_bias).astype(BF)

        if sp_size == 4:
            keyval_all = jnp.zeros((4, tokens, 2 * HD), BF)
            for bit in range(4):
                pairs = [(i, i ^ bit) for i in range(4) if i < i ^ bit]
                piece = lax.ppermute(keyval, "sp", pairs) if bit else keyval
                keyval_all = lax.dynamic_update_slice(keyval_all, piece[None], (spot ^ bit, 0, 0))
            keyval_all = keyval_all.reshape(1, row_len, 2 * HD)
        else:
            keyval_all = lax.all_gather(keyval.reshape(rows, seg, 2 * HD), "sp", axis=1, tiled=True)
        keys, values = keyval_all[:, :, :HD], keyval_all[:, :, HD:]
        keys_t, values_t = keys.transpose(0, 2, 1), values.transpose(0, 2, 1)

        query = (nn(v_first, query_weight) + query_bias).astype(BF).reshape(rows, seg, -1)
        size = min(512, row_len)
        attended, lse = attend_forward(info, query, keys, values_t, size, 4)
        attended_flat = attended.reshape(tokens, -1)

        dmlp_late, _ = lax.optimization_barrier((dmlp, keyval_all))
        dmlp_all = gather_quad(dmlp_late, core)

        proj = tp_sum(nn(attended_flat, output_weight).astype(BF))
        resid = x + proj + output_bias
        hat_two, inv_two = normalize(resid)
        u_second = (hat_two * second_gain + second_bias).astype(BF)
        u_all = gather_quad(u_second, core)

        up_bias_row = up_bias.reshape(1, -1)
        mlp_part, du_part, up_bias_grad = feed_local(u_second, dmlp, up_weight, down_weight, up_bias_row, 512)
        du_second = tp_sum(du_part)
        outputs = (resid + tp_sum(mlp_part) + down_bias).astype(BF).reshape(rows, seg, width)

        dout = dmlp.astype(F32)
        dres_norm, second_gain_grad, second_bias_grad = norm_back(du_second, hat_two, inv_two, second_gain)
        dres = dout + dres_norm
        dproj = dres.astype(BF)
        early = jnp.concatenate(
            [second_gain_grad, second_bias_grad, jnp.sum(dres, axis=0), jnp.sum(dout, axis=0), up_bias_grad[0]]
        )
        early = sum_all(early)

        units = up_weight.shape[1] // 4
        tile = 256
        pieces = 2
        count = units // tile // pieces
        shares = []
        for piece in range(pieces):
            at = ((spot * pieces + piece) * count).astype(jnp.int32).reshape(1)
            part = feed_grads(at, u_all, dmlp_all, up_weight, down_weight, up_bias_row, tile, count)
            share = scatter_rest(part.reshape(dp_size, quads, 4 * shard, -1)).reshape(4, shard, -1)
            blocks = [lax.dynamic_index_in_dim(share, spot ^ bit, 0, keepdims=False) for bit in range(4)]
            shares.append([blocks[0], *[swap(blocks[bit], bit) for bit in range(1, 4)]])
        up_grad = jnp.zeros((4, shard, units), F32)
        down_grad = jnp.zeros((4, shard, units), F32)
        for bit in range(4):
            tiles = [s[bit].astype(F32).reshape(shard, count, 2, tile) for s in shares]
            both = jnp.concatenate(tiles, axis=1)
            up_grad = lax.dynamic_update_slice(up_grad, both[:, :, 0].reshape(1, shard, units), (spot ^ bit, 0, 0))
            down_grad = lax.dynamic_update_slice(down_grad, both[:, :, 1].reshape(1, shard, units), (spot ^ bit, 0, 0))
        up_weight_grad = up_grad.transpose(1, 0, 2).reshape(shard, 4 * units)
        down_weight_grad = down_grad.transpose(0, 2, 1).reshape(4 * units, shard)

        def scatter_rows(value):
            value = value.reshape(dp_size * quads, 4, shard, -1)
            blocks = [
                lax.dynamic_index_in_dim(value, spot ^ bit, 1, keepdims=False).reshape(-1, value.shape[3])
                for bit in range(4)
            ]
            return scatter_rest(scatter_quad(blocks).reshape(dp_size, quads, shard, -1)).astype(F32)

        output_weight_grad = scatter_rows(tn(dproj, attended_flat).astype(BF)).T

        dattended = nt(dproj, output_weight).astype(BF).reshape(rows, seg, -1)
        dquery, dkeyval_part = attend_backward(info, query, dattended, attended, lse, keys, values, keys_t, size, 4)
        dquery = dquery.reshape(tokens, -1)

        if sp_size == 4:
            flat = dkeyval_part.reshape(row_len, 2, HD)
            mine = lax.dynamic_index_in_dim(flat, core, 1, keepdims=False)
            other = lax.dynamic_index_in_dim(flat, 1 - core, 1, keepdims=False)
            half = (mine + swap_tp(other.astype(BF)).astype(F32)).reshape(4, tokens, HD)
            blocks = [lax.dynamic_index_in_dim(half, spot ^ bit, 0, keepdims=False) for bit in range(4)]
            total = blocks[0]
            for bit in range(1, 4):
                pairs = [(i, i ^ bit) for i in range(4) if i > i ^ bit]
                total = total + lax.ppermute(blocks[bit].astype(BF), "sp", pairs).astype(F32)
            own = lax.optimization_barrier(total.astype(BF))
            far = swap_tp(own)
            dkeyval = jnp.where(core == 0, jnp.concatenate([own, far], 1), jnp.concatenate([far, own], 1))
        else:
            part = lax.psum(dkeyval_part.astype(BF), "tp")
            dkeyval = lax.psum_scatter(part, "sp", scatter_dimension=1, tiled=True).reshape(tokens, 2 * HD)
            own = lax.dynamic_slice_in_dim(dkeyval, core * HD, HD, 1)

        query_grad = scatter_rows(jnp.concatenate([tn(v_first, dquery), tn(v_first, own)], axis=1).astype(BF))
        query_weight_grad = query_grad[:, :-HD]
        own_grad = query_grad[:, -HD:]
        far_grad = swap_tp(own_grad)
        keyval_weight_grad = jnp.where(
            core == 0, jnp.concatenate([own_grad, far_grad], 1), jnp.concatenate([far_grad, own_grad], 1)
        )

        dv_first = tp_sum(nt(dquery, query_weight).astype(BF)) + nt(dkeyval, keyval_weight)
        dnorm, first_gain_grad, first_bias_grad = norm_back(dv_first, hat_one, inv_one, first_gain)
        input_grad = (dres + dnorm).astype(BF).reshape(rows, seg, width)
        late = jnp.concatenate(
            [
                first_gain_grad,
                first_bias_grad,
                jnp.sum(dquery.astype(F32), axis=0),
                jnp.sum(dkeyval[:, HD:].astype(F32), axis=0),
            ]
        )
        late = sum_all(late)
        heads_wide = query_bias.shape[0]
        return (
            outputs,
            input_grad,
            late[:width],
            late[width : 2 * width],
            query_weight_grad,
            late[2 * width : 2 * width + heads_wide],
            keyval_weight_grad,
            late[2 * width + heads_wide :],
            output_weight_grad,
            early[2 * width : 3 * width],
            early[:width],
            early[width : 2 * width],
            up_weight_grad,
            early[4 * width :],
            down_weight_grad,
            early[3 * width : 4 * width],
        )

    return per_device


def solution(mesh):
    placed = (
        P("dp", "sp", None),
        P("dp"),
        P(),
        P(),
        P(None, "tp"),
        P("tp"),
        P(),
        P(),
        P("tp", None),
        P(),
        P(),
        P(),
        P(None, "tp"),
        P("tp"),
        P("tp", None),
        P(),
        P("dp", "sp", None),
    )
    return jax.shard_map(
        build(mesh),
        mesh=mesh,
        in_specs=placed,
        out_specs=(
            P("dp", "sp", None),
            P("dp", "sp", None),
            P(),
            P(),
            P(("dp", "sp"), "tp"),
            P("tp"),
            P(("dp", "sp"), None),
            P(),
            P("tp", ("dp", "sp")),
            P(),
            P(),
            P(),
            P(("dp", "sp"), "tp"),
            P("tp"),
            P("tp", ("dp", "sp")),
            P(),
        ),
        check_vma=False,
    )
```

time: 1590 us -> 650 us (0.41)
  waiting for transfers between devices: 1090 us -> 180 us
  matrix products: 205 us -> 33.7 us
  Pallas kernels: 0 us -> 123 us
  other arithmetic: 112 us -> 50.5 us
  starting transfers between devices: 23.4 us -> 81 us
  local copies, waits for them, and re-layouts: 115 us -> 158 us
  blocking collectives: 17.9 us -> 0 us
    reduce_scatter x8 -> x3, waiting for transfers between devices: 789 us -> 67.6 us  [scatter_rest(): lax.psum_scatter(value.reshape(-1, columns), 'dp', scatter_dimension=0, t...]
    psum x4 -> x0, waiting for transfers between devices: 188 us -> none  [the longest x1 114 us: per_device(): lax.psum((first_gain_grad, first_bias_grad, query_bias_grad, value_bias_g...]
    dot_general x39 -> x9, matrix products: 205 us -> 33.7 us  [the longest x3 14.1 us: nt(): lax.dot_general(left, right, (((1,), (1,)), ((), ())), preferred_element_...]
    pallas_call x0 -> x5, Pallas kernels: none -> 123 us  [the longest x2 58.1 us: feed_grads(): pl.pallas_call(grad_kernel, grid_spec=pltpu.PrefetchScalarGridSpec(num_sc...]
    ppermute x0 -> x55, waiting for transfers between devices: none -> 112 us  [the longest x30 93.1 us: swap(): return lax.ppermute(value, 'sp', [(i, i ^ bit) for i in range(sp_size)])]
    unnamed x16 -> x5, waiting for transfers between devices: 84.7 us -> 0.07 us
    ppermute x0 -> x55, starting transfers between devices: none -> 80.9 us  [the longest x30 49.4 us: swap(): return lax.ppermute(value, 'sp', [(i, i ^ bit) for i in range(sp_size)])]
    unnamed x6 -> x1, other arithmetic: 50.5 us -> 2.15 us
  transfers between devices with their start and end apart: 19 -> 59, of which waited for: 16 -> 18; matrix products, arithmetic and copies ran while one was open for 9% -> 29% of each run, Pallas kernels for 0% -> 19%
where the time goes in v1:
time: 650 us; the launch traced here: 641 us
  waiting for transfers between devices  180 us (28%)
  local copies, waits for them, and re-layouts  158 us (24%)
  Pallas kernels  123 us (19%)
  starting transfers between devices  81 us (12%)
  other arithmetic  50.5 us (8%)
  matrix products  33.7 us (5%)
  between operations  15.6 us (2%)
    ppermute x30, waiting for transfers between devices, swap(): return lax.ppermute(value, 'sp', [(i, i ^ bit) for i in range(sp_size)])  93.1 us
    reduce_scatter x3, waiting for transfers between devices, scatter_rest(): lax.psum_scatter(value.reshape(-1, columns), 'dp', scatter_dimension=0, t...  67.6 us
    pallas_call x2, Pallas kernels, feed_grads(): pl.pallas_call(grad_kernel, grid_spec=pltpu.PrefetchScalarGridSpec(num_sc...  58.1 us
    ppermute x30, starting transfers between devices, swap(): return lax.ppermute(value, 'sp', [(i, i ^ bit) for i in range(sp_size)])  49.4 us
    pallas_call x1, Pallas kernels, feed_local(): pl.pallas_call(local_kernel, grid=(units // tile,), in_specs=[whole, whol...  45.1 us
    dynamic_update_slice x4, local copies, waits for them, and re-layouts, per_device(): lax.dynamic_update_slice(keyval_all, piece[None], (spot ^ bit, 0, 0))  41 us
    unnamed x101, local copies, waits for them, and re-layouts  35.7 us
    ppermute x4, waiting for transfers between devices, swap_dp(): return lax.ppermute(value, 'dp', [(i, i ^ bit) for i in range(dp_size)])  15.3 us
  transfers between devices with their start and end apart: 59, of which 18 were waited for; matrix products, arithmetic and copies ran while one was open for 29% of the time, Pallas kernels for 19%

profile of v1, /device:TPU:0, one launch (start us, length us, event | category | flops | bytes accessed | tf_op | source)
XLA Modules:
  0.0 641.4 jit_solution(4998849132049012871)
XLA Ops:
  7.3 2.1 convert_reduce_fusion
  9.4 2.3 fusion.16
  13.4 5.6 collective-permute-start
  18.9 4.1 collective-permute-start.1
  25.0 3.4 fusion.29.q_ref
  31.6 10.3 %dynamic_update_slice.36 = bf16[4,512,256]{1,0,2:T(4,128)(2,1)} dynamic-update-slice(bf16[4,512,256]{1,0,2:T(4,128)(2,1)} %broadcast_in_dim.10, bf16[1,512,256]{1,0,2:T(2,128)(2,1)} %copy.81, s32[]{:T(128)S(6)} %select_n.71, s32[]{:T(128)} %constant.92.clone.1, s32[]{:T(128)} %constant.92.clone.1) | dynamic-update-slice | bytes 524292 | tf_op jit(solution)/shard_map/dynamic_update_slice | solution.py:363
  48.3 10.3 %dynamic_update_slice.37 = bf16[4,512,256]{1,0,2:T(4,128)(2,1)} dynamic-update-slice(bf16[4,512,256]{1,0,2:T(4,128)(2,1)} %dynamic_update_slice.36, bf16[1,512,256]{1,0,2:T(2,128)(2,1)} %copy.82, s32[]{:T(128)S(6)} %select_n.72, s32[]{:T(128)} %constant.92.clone.1, s32[]{:T(128)} %constant.92.clone.1) | dynamic-update-slice | bytes 524292 | tf_op jit(solution)/shard_map/dynamic_update_slice | solution.py:363
  58.6 10.3 %dynamic_update_slice.38 = bf16[4,512,256]{1,0,2:T(4,128)(2,1)} dynamic-update-slice(bf16[4,512,256]{1,0,2:T(4,128)(2,1)} %dynamic_update_slice.37, bf16[1,512,256]{1,0,2:T(2,128)(2,1)} %copy.83, s32[]{:T(128)S(6)} %select_n.73, s32[]{:T(128)} %constant.92.clone.1, s32[]{:T(128)} %constant.92.clone.1) | dynamic-update-slice | bytes 524292 | tf_op jit(solution)/shard_map/dynamic_update_slice | solution.py:363
  68.8 10.3 %dynamic_update_slice.39 = bf16[4,512,256]{1,0,2:T(4,128)(2,1)} dynamic-update-slice(bf16[4,512,256]{1,0,2:T(4,128)(2,1)} %dynamic_update_slice.38, bf16[1,512,256]{1,0,2:T(2,128)(2,1)} %copy.84, s32[]{:T(128)S(6)} %select_n.74, s32[]{:T(128)} %constant.92.clone.1, s32[]{:T(128)} %constant.92.clone.1) | dynamic-update-slice | bytes 524292 | tf_op jit(solution)/shard_map/dynamic_update_slice | solution.py:363
  79.1 2.6 reshape.255
  81.7 2.6 slice_bitcast_fusion.1
  84.3 2.3 constant_dynamic-slice_fusion.9
  89.5 7.9 %attend_forward.1 = (bf16[1,512,1024]{2,1,0:T(8,128)(2,1)}, f32[1,2,1,2048]{3,2,1,0:T(1,128)}) custom-call(s32[2]{0:T(128)} %pad_add_fusion.info_ref, bf16[1,512,1024]{2,1,0:T(8,128)(2,1)} %fusion.29.q_ref, bf16[1,2048,128]{2,1,0:T(8,128)(2,1)} %copy.85.k_ref, bf16[1,128,2048]{2,1,0:T(8,128)(2,1)} %get-tuple-element.91.vt_ref), custom_call_target="tpu_custom_call" | custom-call | flops 8000000000 | bytes 4194304 | tf_op jit(solution)/shard_map/attend_forward/pallas_call | solution.py:92
  97.4 6.2 convolution_convert_fusion.2
  103.6 2.2 fusion.26
  105.7 3.9 copy.113
  109.7 2.2 fusion.79
  111.8 4.1 copy.114
  117.8 9.9 %collective-permute-start.43 = (bf16[128,2048]{1,0:T(8,128)(2,1)}, bf16[128,2048]{1,0:T(8,128)(2,1)}, u32[]{:S(2)}, u32[]{:S(2)}) collective-permute-start(bf16[128,2048]{1,0:T(8,128)(2,1)} %slice.230), channel_id=1, source_target_pairs={{0,4},{2,6},{4,0},{6,2},{1,5},{3,7},{5,1},{7,3},{8,12},{10,14},{12... | collective-permute-start | bytes 1572872 | tf_op jit(solution)/shard_map/ppermute | solution.py:291
  127.7 3.1 constant_dynamic-update-slice_fusion.18
  136.6 2.3 constant_dynamic-update-slice_fusion.17
  138.9 2.4 constant_dynamic-update-slice_fusion.16
  143.2 3.2 fusion.56
  147.2 2.1 constant_dynamic-update-slice_fusion.9
  151.3 45.1 %feed_local.1 = (bf16[512,2048]{1,0:T(8,128)(2,1)}, bf16[512,2048]{1,0:T(8,128)(2,1)}, f32[1,4096]{1,0:T(1,128)}) custom-call(bf16[512,2048]{1,0:T(8,128)(2,1)} %copy-done.10, bf16[512,2048]{1,0:T(8,128)(2,1)} %bitcast.194, bf16[2048,4096]{1,0:T(8,128)(2,1)} %up_ref.5, bf16[4096,2048]{1,0:T(8,128)(2,1)} %down_ref.5, f32[1,4096]{1,0:T(1,128)} %bitcast.225), custom_call_target="tpu_custom_call" | custom-call | flops 34359738368 | bytes 33554432 | tf_op jit(solution)/shard_map/feed_local/pallas_call | solution.py:211
  200.4 2.3 constant_dynamic-update-slice_fusion.13
  202.7 2.3 constant_dynamic-update-slice_fusion.12
  209.5 13.2 %collective-permute-done.34 = bf16[256,2048]{1,0:T(8,128)(2,1)S(1)} collective-permute-done((bf16[256,2048]{1,0:T(8,128)(2,1)}, bf16[256,2048]{1,0:T(8,128)(2,1)S(1)}, u32[]{:S(2)}, u32[]{:S(2)}) %collective-permute-start.34) | collective-permute-done | bytes 1048608 | tf_op jit(solution)/shard_map/ppermute | solution.py:291
  224.1 2.3 constant_dynamic-update-slice_fusion.8
  227.4 5.9 collective-permute-done.35
  237.4 2.5 multiply_reduce_fusion
  239.9 5.1 fusion.55
  245.1 3.4 fusion.28.do_ref
  248.4 4.4 convolution_convert_fusion
  252.9 11.6 %attend_backward.1 = (bf16[1,512,1024]{2,1,0:T(8,128)(2,1)}, f32[1,2048,256]{2,1,0:T(8,128)}) custom-call(s32[2]{0:T(128)} %pad_add_fusion.info_ref, bf16[1,512,1024]{2,1,0:T(8,128)(2,1)} %fusion.29.q_ref, bf16[1,512,1024]{2,1,0:T(8,128)(2,1)} %fusion.28.do_ref, bf16[1,512,1024]{2,1,0:T(8,128)(2,1)} %get-tuple-element.24.o_ref, ...), custom_call_target="tpu_custom_call" | custom-call | flops 16000000000 | bytes 8388608 | tf_op jit(solution)/shard_map/attend_backward/pallas_call | solution.py:152
  264.4 2.3 reshape.262
  266.7 2.8 constant_dynamic-slice_fusion.18
  274.8 12.0 %collective-permute-start.27 = (bf16[256,1024]{0,1:T(8,128)(2,1)}, bf16[256,1024]{0,1:T(8,128)(2,1)}, u32[]{:S(2)}, u32[]{:S(2)}) collective-permute-start(bf16[256,1024]{0,1:T(8,128)(2,1)} %copy.123), channel_id=1, source_target_pairs={{0,4},{2,6},{4,0},{6,2},{1,5},{3,7},{5,1},{7,3},{8,12},{10,14},{12... | collective-permute-start | bytes 1572872 | tf_op jit(solution)/shard_map/ppermute | solution.py:291
  296.7 2.1 bitcast_convert_fusion.3
  300.4 2.1 copy.117
  302.5 4.3 convolution_convert_fusion.3
  320.4 3.2 collective-permute-start.25
  328.4 13.3 %collective-permute-done.28 = bf16[256,1024]{0,1:T(8,128)(2,1)S(1)} collective-permute-done((bf16[256,1024]{0,1:T(8,128)(2,1)S(1)}, bf16[256,1024]{0,1:T(8,128)(2,1)S(1)}, u32[]{:S(2)}, u32[]{:S(2)}) %collective-permute-start.28) | collective-permute-done | bytes 524320 | tf_op jit(solution)/shard_map/ppermute | solution.py:291
  341.7 3.1 collective-permute-start.19
  351.6 11.1 %collective-permute-done.17 = bf16[256,1152]{1,0:T(8,128)(2,1)} collective-permute-done((bf16[256,1152]{1,0:T(8,128)(2,1)}, bf16[256,1152]{1,0:T(8,128)(2,1)}, u32[]{:S(2)}, u32[]{:S(2)}) %collective-permute-start.17) | collective-permute-done | bytes 589856 | tf_op jit(solution)/shard_map/ppermute | solution.py:291
  364.4 21.0 %collective-permute-done.21 = bf16[256,1152]{1,0:T(8,128)(2,1)S(1)} collective-permute-done((bf16[256,1152]{1,0:T(8,128)(2,1)S(1)}, bf16[256,1152]{1,0:T(8,128)(2,1)S(1)}, u32[]{:S(2)}, u32[]{:S(2)}) %collective-permute-start.21) | collective-permute-done | bytes 589856 | tf_op jit(solution)/shard_map/ppermute | solution.py:291
  389.7 2.3 constant_dynamic-update-slice_fusion.4
  397.0 28.9 %feed_grads.3 = bf16[2048,1024]{1,0:T(8,128)(2,1)} custom-call(s32[1]{0:T(128)} %bitcast.53.at_ref, bf16[2048,2048]{1,0:T(8,128)(2,1)} %constant_dynamic-update-slice_fusion.1.u_ref, bf16[2048,2048]{1,0:T(8,128)(2,1)} %constant_dynamic-update-slice_fusion.10.dm_ref, bf16[2048,4096]{1,0:T(8,128)(2,1)} %up_ref.5, bf16[4096,2048]{1,0:T(8,128)(2,1)} %down_ref.5, ...), custom_call_target="tpu_custom_call" | custom-call | flops 17179869184 | bytes 25165824 | tf_op jit(solution)/shard_map/feed_grads/pallas_call | solution.py:247
  426.0 29.1 %feed_grads.2 = bf16[2048,1024]{1,0:T(8,128)(2,1)} custom-call(s32[1]{0:T(128)} %bitcast.50.at_ref, bf16[2048,2048]{1,0:T(8,128)(2,1)} %constant_dynamic-update-slice_fusion.1.u_ref, bf16[2048,2048]{1,0:T(8,128)(2,1)} %constant_dynamic-update-slice_fusion.10.dm_ref, bf16[2048,4096]{1,0:T(8,128)(2,1)} %up_ref.5, bf16[4096,2048]{1,0:T(8,128)(2,1)} %down_ref.5, ...), custom_call_target="tpu_custom_call" | custom-call | flops 17179869184 | bytes 25165824 | tf_op jit(solution)/shard_map/feed_grads/pallas_call | solution.py:247
  455.3 6.3 convolution_convert_fusion.1
  461.8 4.0 collective-permute-done.29
  466.0 4.0 collective-permute-done.30
  470.1 6.4 collective-permute-done.31
  476.5 11.0 %collective-permute-start.32 = (f32[12288]{0:T(1024)S(1)}, f32[12288]{0:T(1024)S(1)}, u32[]{:S(2)}, u32[]{:S(2)}) collective-permute-start(f32[12288]{0:T(1024)S(1)} %add.290), channel_id=1, source_target_pairs={{0,16},{8,24},{16,0},{24,8},{1,17},{9,25},{17,1},{25,9},{2,18},{10... | collective-permute-start | bytes 147464 | tf_op jit(solution)/shard_map/ppermute | solution.py:294
  488.9 5.2 collective-permute-done.32
  494.4 4.4 fusion.15
  503.5 3.0 collective-permute-done.13
  507.6 3.7 collective-permute-done.14
  511.3 2.1 collective-permute-start.15
  513.4 2.7 fusion.27
  524.6 67.6 %reduce-scatter.9.cloned.1.call-done = bf16[512,1024]{1,0:T(8,128)(2,1)} async-done(((bf16[2048,1024]{1,0:T(8,128)(2,1)}), bf16[512,1024]{1,0:T(8,128)(2,1)}) %reduce-scatter.9.cloned.1.call-update) | async-done | bytes 1048592 | tf_op jit(solution)/shard_map/reduce_scatter | solution.py:333
  602.2 2.5 collective-permute-start.54
  607.2 2.4 collective-permute-done.49
  610.8 13.0 %collective-permute-done.51 = bf16[128,1024]{0,1:T(8,128)(2,1)} collective-permute-done((bf16[128,1024]{0,1:T(8,128)(2,1)}, bf16[128,1024]{0,1:T(8,128)(2,1)}, u32[]{:S(2)}, u32[]{:S(2)}) %collective-permute-start.51) | collective-permute-done | bytes 262176 | tf_op jit(solution)/shard_map/ppermute | solution.py:291
  (298 shorter events, 135.9 us)
Async XLA Ops:
  7.2 510.6 %reduce-scatter.13.cloned.1.call-start = ((), (), s32[]{:S(2)}) async-start(), calls=%async_computation.7 | async-start | bytes 1310720
  9.4 100.3 %copy-start.24 = (f32[512]{0:T(512)}, f32[512]{0:T(512)S(1)}, u32[]{:S(2)}) copy-start(f32[512]{0:T(512)S(1)} %broadcast_multiply_fusion.5) | copy-start | bytes 6148
  11.7 97.9 %copy-start.28 = (f32[512]{0:T(512)}, f32[512]{0:T(512)S(1)}, u32[]{:S(2)}) copy-start(f32[512]{0:T(512)S(1)} %add_rsqrt_fusion.1) | copy-start | bytes 6148
  13.4 29.1 %collective-permute-start = (bf16[512,256]{1,0:T(8,128)(2,1)S(1)}, bf16[512,256]{1,0:T(8,128)(2,1)}, u32[]{:S(2)}, u32[]{:S(2)}) collective-permute-start(bf16[512,256]{1,0:T(8,128)(2,1)S(1)} %fusion.30), channel_id=1, source_target_pairs={{0,2},{4,6},{1,3},{5,7},{8,10},{12,14},{9,11},{13,15},{16,18},{20,... | collective-permute-start | bytes 786440 | tf_op jit(solution)/shard_map/ppermute | solution.py:362
  18.9 25.5 %collective-permute-start.1 = (bf16[512,256]{1,0:T(8,128)(2,1)S(1)}, bf16[512,256]{1,0:T(8,128)(2,1)}, u32[]{:S(2)}, u32[]{:S(2)}) collective-permute-start(bf16[512,256]{1,0:T(8,128)(2,1)S(1)} %fusion.30), channel_id=1, source_target_pairs={{0,4},{2,6},{1,5},{3,7},{8,12},{10,14},{9,13},{11,15},{16,20},{18,... | collective-permute-start | bytes 786440 | tf_op jit(solution)/shard_map/ppermute | solution.py:362
  23.0 23.3 %collective-permute-start.2 = (bf16[512,256]{1,0:T(8,128)(2,1)S(1)}, bf16[512,256]{1,0:T(8,128)(2,1)}, u32[]{:S(2)}, u32[]{:S(2)}) collective-permute-start(bf16[512,256]{1,0:T(8,128)(2,1)S(1)} %fusion.30), channel_id=1, source_target_pairs={{0,6},{2,4},{1,7},{3,5},{8,14},{10,12},{9,15},{11,13},{16,22},{18,... | collective-permute-start | bytes 786440 | tf_op jit(solution)/shard_map/ppermute | solution.py:362
  86.6 29.3 %collective-permute-start.41 = (bf16[256,2048]{1,0:T(8,128)(2,1)}, bf16[256,2048]{1,0:T(8,128)(2,1)}, u32[]{:S(2)}, u32[]{:S(2)}) collective-permute-start(bf16[256,2048]{1,0:T(8,128)(2,1)} %constant_dynamic-slice_fusion.9), channel_id=1, source_target_pairs={{0,2},{2,0},{4,6},{6,4},{1,3},{3,1},{5,7},{7,5},{8,10},{10,8},{12,... | collective-permute-start | bytes 3145736 | tf_op jit(solution)/shard_map/ppermute | solution.py:291
  87.4 45.5 %collective-permute-start.42 = (bf16[256,2048]{1,0:T(8,128)(2,1)}, bf16[256,2048]{1,0:T(8,128)(2,1)}, u32[]{:S(2)}, u32[]{:S(2)}) collective-permute-start(bf16[256,2048]{1,0:T(8,128)(2,1)} %constant_dynamic-slice_fusion.9), channel_id=1, source_target_pairs={{0,4},{2,6},{4,0},{6,2},{1,5},{3,7},{5,1},{7,3},{8,12},{10,14},{12... | collective-permute-start | bytes 3145736 | tf_op jit(solution)/shard_map/ppermute | solution.py:291
  103.5 39.7 %collective-permute-start.3 = (bf16[512,2048]{1,0:T(8,128)(2,1)}, bf16[512,2048]{1,0:T(8,128)(2,1)}, u32[]{:S(2)}, u32[]{:S(2)}) collective-permute-start(bf16[512,2048]{1,0:T(8,128)(2,1)} %convolution_convert_fusion.2), channel_id=1, source_target_pairs={{0,1},{1,0},{2,3},{3,2},{4,5},{5,4},{6,7},{7,6},{8,9},{9,8},{10,11... | collective-permute-start | bytes 6291464 | tf_op jit(solution)/shard_map/ppermute | solution.py:297
  117.8 23.5 %collective-permute-start.43 = (bf16[128,2048]{1,0:T(8,128)(2,1)}, bf16[128,2048]{1,0:T(8,128)(2,1)}, u32[]{:S(2)}, u32[]{:S(2)}) collective-permute-start(bf16[128,2048]{1,0:T(8,128)(2,1)} %slice.230), channel_id=1, source_target_pairs={{0,4},{2,6},{4,0},{6,2},{1,5},{3,7},{5,1},{7,3},{8,12},{10,14},{12... | collective-permute-start | bytes 1572872 | tf_op jit(solution)/shard_map/ppermute | solution.py:291
  134.9 61.6 %collective-permute-start.44 = (bf16[128,2048]{1,0:T(8,128)(2,1)}, bf16[128,2048]{1,0:T(8,128)(2,1)}, u32[]{:S(2)}, u32[]{:S(2)}) collective-permute-start(bf16[128,2048]{1,0:T(8,128)(2,1)} %slice.231), channel_id=1, source_target_pairs={{0,2},{2,0},{4,6},{6,4},{1,3},{3,1},{5,7},{7,5},{8,10},{10,8},{12,... | collective-permute-start | bytes 1572872 | tf_op jit(solution)/shard_map/ppermute | solution.py:291
  136.1 61.9 %collective-permute-start.45 = (bf16[256,2048]{1,0:T(8,128)(2,1)}, bf16[256,2048]{1,0:T(8,128)(2,1)}, u32[]{:S(2)}, u32[]{:S(2)}) collective-permute-start(bf16[256,2048]{1,0:T(8,128)(2,1)} %collective-permute-done.41), channel_id=1, source_target_pairs={{0,1},{1,0},{2,3},{3,2},{4,5},{5,4},{6,7},{7,6},{8,9},{9,8},{10,11... | collective-permute-start | bytes 3145736 | tf_op jit(solution)/shard_map/ppermute | solution.py:297
  136.1 63.8 %collective-permute-start.46 = (bf16[256,2048]{1,0:T(8,128)(2,1)}, bf16[256,2048]{1,0:T(8,128)(2,1)}, u32[]{:S(2)}, u32[]{:S(2)}) collective-permute-start(bf16[256,2048]{1,0:T(8,128)(2,1)} %collective-permute-done.42), channel_id=1, source_target_pairs={{0,1},{1,0},{2,3},{3,2},{4,5},{5,4},{6,7},{7,6},{8,9},{9,8},{10,11... | collective-permute-start | bytes 3145736 | tf_op jit(solution)/shard_map/ppermute | solution.py:297
  141.3 63.7 %collective-permute-start.47 = (bf16[128,2048]{1,0:T(8,128)(2,1)}, bf16[128,2048]{1,0:T(8,128)(2,1)}, u32[]{:S(2)}, u32[]{:S(2)}) collective-permute-start(bf16[128,2048]{1,0:T(8,128)(2,1)} %collective-permute-done.43), channel_id=1, source_target_pairs={{0,1},{1,0},{2,3},{3,2},{4,5},{5,4},{6,7},{7,6},{8,9},{9,8},{10,11... | collective-permute-start | bytes 1572872 | tf_op jit(solution)/shard_map/ppermute | solution.py:297
  150.6 56.4 %collective-permute-start.33 = (bf16[256,2048]{1,0:T(8,128)(2,1)}, bf16[256,2048]{1,0:T(8,128)(2,1)}, u32[]{:S(2)}, u32[]{:S(2)}) collective-permute-start(bf16[256,2048]{1,0:T(8,128)(2,1)} %constant_dynamic-slice_fusion.10), channel_id=1, source_target_pairs={{0,2},{2,0},{4,6},{6,4},{1,3},{3,1},{5,7},{7,5},{8,10},{10,8},{12,... | collective-permute-start | bytes 3145736 | tf_op jit(solution)/shard_map/ppermute | solution.py:291
  196.4 26.3 %collective-permute-start.34 = (bf16[256,2048]{1,0:T(8,128)(2,1)}, bf16[256,2048]{1,0:T(8,128)(2,1)S(1)}, u32[]{:S(2)}, u32[]{:S(2)}) collective-permute-start(bf16[256,2048]{1,0:T(8,128)(2,1)} %constant_dynamic-slice_fusion.10), channel_id=1, source_target_pairs={{0,4},{2,6},{4,0},{6,2},{1,5},{3,7},{5,1},{7,3},{8,12},{10,14},{12... | collective-permute-start | bytes 3145736 | tf_op jit(solution)/shard_map/ppermute | solution.py:291
  198.0 39.3 %collective-permute-start.5 = (bf16[512,2048]{1,0:T(8,128)(2,1)}, bf16[512,2048]{1,0:T(8,128)(2,1)S(1)}, u32[]{:S(2)}, u32[]{:S(2)}) collective-permute-start(bf16[512,2048]{1,0:T(8,128)(2,1)} %get-tuple-element.26), channel_id=1, source_target_pairs={{0,1},{1,0},{2,3},{3,2},{4,5},{5,4},{6,7},{7,6},{8,9},{9,8},{10,11... | collective-permute-start | bytes 6291464 | tf_op jit(solution)/shard_map/ppermute | solution.py:297
  199.9 8.8 %collective-permute-start.48 = (bf16[128,2048]{1,0:T(8,128)(2,1)}, bf16[128,2048]{1,0:T(8,128)(2,1)S(1)}, u32[]{:S(2)}, u32[]{:S(2)}) collective-permute-start(bf16[128,2048]{1,0:T(8,128)(2,1)} %collective-permute-done.44), channel_id=1, source_target_pairs={{0,1},{1,0},{2,3},{3,2},{4,5},{5,4},{6,7},{7,6},{8,9},{9,8},{10,11... | collective-permute-start | bytes 1572872 | tf_op jit(solution)/shard_map/ppermute | solution.py:297
  205.0 34.8 %collective-permute-start.4 = (bf16[512,2048]{1,0:T(8,128)(2,1)S(1)}, bf16[512,2048]{1,0:T(8,128)(2,1)S(1)}, u32[]{:S(2)}, u32[]{:S(2)}) collective-permute-start(bf16[512,2048]{1,0:T(8,128)(2,1)S(1)} %copy-done.17), channel_id=1, source_target_pairs={{0,1},{1,0},{2,3},{3,2},{4,5},{5,4},{6,7},{7,6},{8,9},{9,8},{10,11... | collective-permute-start | bytes 6291464 | tf_op jit(solution)/shard_map/ppermute | solution.py:297
  208.1 25.3 %collective-permute-start.35 = (bf16[128,2048]{1,0:T(8,128)(2,1)S(1)}, bf16[128,2048]{1,0:T(8,128)(2,1)}, u32[]{:S(2)}, u32[]{:S(2)}) collective-permute-start(bf16[128,2048]{1,0:T(8,128)(2,1)S(1)} %slice.228), channel_id=1, source_target_pairs={{0,4},{2,6},{4,0},{6,2},{1,5},{3,7},{5,1},{7,3},{8,12},{10,14},{12... | collective-permute-start | bytes 1572872 | tf_op jit(solution)/shard_map/ppermute | solution.py:291
  222.8 12.7 %collective-permute-start.36 = (bf16[128,2048]{1,0:T(8,128)(2,1)S(1)}, bf16[128,2048]{1,0:T(8,128)(2,1)}, u32[]{:S(2)}, u32[]{:S(2)}) collective-permute-start(bf16[128,2048]{1,0:T(8,128)(2,1)S(1)} %slice.229), channel_id=1, source_target_pairs={{0,2},{2,0},{4,6},{6,4},{1,3},{3,1},{5,7},{7,5},{8,10},{10,8},{12,... | collective-permute-start | bytes 1572872 | tf_op jit(solution)/shard_map/ppermute | solution.py:291
  224.1 165.7 %collective-permute-start.37 = (bf16[256,2048]{1,0:T(8,128)(2,1)}, bf16[256,2048]{1,0:T(8,128)(2,1)}, u32[]{:S(2)}, u32[]{:S(2)}) collective-permute-start(bf16[256,2048]{1,0:T(8,128)(2,1)} %collective-permute-done.33), channel_id=1, source_target_pairs={{0,1},{1,0},{2,3},{3,2},{4,5},{5,4},{6,7},{7,6},{8,9},{9,8},{10,11... | collective-permute-start | bytes 3145736 | tf_op jit(solution)/shard_map/ppermute | solution.py:297
  270.4 36.5 %collective-permute-start.7 = (bf16[2048,128]{1,0:T(8,128)(2,1)}, bf16[2048,128]{1,0:T(8,128)(2,1)}, u32[]{:S(2)}, u32[]{:S(2)}) collective-permute-start(bf16[2048,128]{1,0:T(8,128)(2,1)} %convert_bitcast_fusion.2), channel_id=1, source_target_pairs={{0,1},{1,0},{2,3},{3,2},{4,5},{5,4},{6,7},{7,6},{8,9},{9,8},{10,11... | collective-permute-start | bytes 1572872 | tf_op jit(solution)/shard_map/ppermute | solution.py:297
  274.8 34.7 %collective-permute-start.27 = (bf16[256,1024]{0,1:T(8,128)(2,1)}, bf16[256,1024]{0,1:T(8,128)(2,1)}, u32[]{:S(2)}, u32[]{:S(2)}) collective-permute-start(bf16[256,1024]{0,1:T(8,128)(2,1)} %copy.123), channel_id=1, source_target_pairs={{0,4},{2,6},{4,0},{6,2},{1,5},{3,7},{5,1},{7,3},{8,12},{10,14},{12... | collective-permute-start | bytes 1572872 | tf_op jit(solution)/shard_map/ppermute | solution.py:291
  291.3 37.0 %collective-permute-start.26 = (bf16[256,1024]{0,1:T(8,128)(2,1)}, bf16[256,1024]{0,1:T(8,128)(2,1)}, u32[]{:S(2)}, u32[]{:S(2)}) collective-permute-start(bf16[256,1024]{0,1:T(8,128)(2,1)} %copy.121), channel_id=1, source_target_pairs={{0,4},{2,6},{4,0},{6,2},{1,5},{3,7},{5,1},{7,3},{8,12},{10,14},{12... | collective-permute-start | bytes 1572872 | tf_op jit(solution)/shard_map/ppermute | solution.py:291
  295.9 16.1 %collective-permute-start.24 = (bf16[256,1024]{0,1:T(8,128)(2,1)}, bf16[256,1024]{0,1:T(8,128)(2,1)}, u32[]{:S(2)}, u32[]{:S(2)}) collective-permute-start(bf16[256,1024]{0,1:T(8,128)(2,1)} %copy.119), channel_id=1, source_target_pairs={{0,2},{2,0},{4,6},{6,4},{1,3},{3,1},{5,7},{7,5},{8,10},{10,8},{12,... | collective-permute-start | bytes 1572872 | tf_op jit(solution)/shard_map/ppermute | solution.py:291
  308.2 8.2 %collective-permute-start.10 = (bf16[512,128]{1,0:T(8,128)(2,1)S(1)}, bf16[512,128]{1,0:T(8,128)(2,1)S(1)}, u32[]{:S(2)}, u32[]{:S(2)}) collective-permute-start(bf16[512,128]{1,0:T(8,128)(2,1)S(1)} %get-tuple-element.88), channel_id=1, source_target_pairs={{4,2},{6,0},{5,3},{7,1},{12,10},{14,8},{13,11},{15,9},{20,18},{22,... | collective-permute-start | bytes 393224 | tf_op jit(solution)/shard_map/ppermute | solution.py:442
  309.5 9.6 %collective-permute-start.9 = (bf16[512,128]{1,0:T(8,128)(2,1)S(1)}, bf16[512,128]{1,0:T(8,128)(2,1)S(1)}, u32[]{:S(2)}, u32[]{:S(2)}) collective-permute-start(bf16[512,128]{1,0:T(8,128)(2,1)S(1)} %get-tuple-element.89), channel_id=1, source_target_pairs={{4,0},{6,2},{5,1},{7,3},{12,8},{14,10},{13,9},{15,11},{20,16},{22,... | collective-permute-start | bytes 393224 | tf_op jit(solution)/shard_map/ppermute | solution.py:442
  312.0 8.4 %collective-permute-start.8 = (bf16[512,128]{1,0:T(8,128)(2,1)S(1)}, bf16[512,128]{1,0:T(8,128)(2,1)S(1)}, u32[]{:S(2)}, u32[]{:S(2)}) collective-permute-start(bf16[512,128]{1,0:T(8,128)(2,1)S(1)} %get-tuple-element.87), channel_id=1, source_target_pairs={{2,0},{6,4},{3,1},{7,5},{10,8},{14,12},{11,9},{15,13},{18,16},{22,... | collective-permute-start | bytes 393224 | tf_op jit(solution)/shard_map/ppermute | solution.py:442
  316.4 29.6 %collective-permute-start.23 = (bf16[256,1024]{0,1:T(8,128)(2,1)S(1)}, bf16[256,1024]{0,1:T(8,128)(2,1)S(1)}, u32[]{:S(2)}, u32[]{:S(2)}) collective-permute-start(bf16[256,1024]{0,1:T(8,128)(2,1)S(1)} %copy-done.20), channel_id=1, source_target_pairs={{0,2},{2,0},{4,6},{6,4},{1,3},{3,1},{5,7},{7,5},{8,10},{10,8},{12,... | collective-permute-start | bytes 1572872 | tf_op jit(solution)/shard_map/ppermute | solution.py:291
  319.2 22.5 %collective-permute-start.28 = (bf16[256,1024]{0,1:T(8,128)(2,1)S(1)}, bf16[256,1024]{0,1:T(8,128)(2,1)S(1)}, u32[]{:S(2)}, u32[]{:S(2)}) collective-permute-start(bf16[256,1024]{0,1:T(8,128)(2,1)S(1)} %add_convert_fusion.4), channel_id=1, source_target_pairs={{0,2},{2,0},{4,6},{6,4},{1,3},{3,1},{5,7},{7,5},{8,10},{10,8},{12,... | collective-permute-start | bytes 1572872 | tf_op jit(solution)/shard_map/ppermute | solution.py:291
  320.4 25.9 %collective-permute-start.25 = (bf16[256,1024]{0,1:T(8,128)(2,1)S(1)}, bf16[256,1024]{0,1:T(8,128)(2,1)S(1)}, u32[]{:S(2)}, u32[]{:S(2)}) collective-permute-start(bf16[256,1024]{0,1:T(8,128)(2,1)S(1)} %add_convert_fusion.6), channel_id=1, source_target_pairs={{0,4},{2,6},{4,0},{6,2},{1,5},{3,7},{5,1},{7,3},{8,12},{10,14},{12... | collective-permute-start | bytes 1572872 | tf_op jit(solution)/shard_map/ppermute | solution.py:291
  328.4 21.5 %collective-permute-start.20 = (bf16[256,1152]{1,0:T(8,128)(2,1)}, bf16[256,1152]{1,0:T(8,128)(2,1)}, u32[]{:S(2)}, u32[]{:S(2)}) collective-permute-start(bf16[256,1152]{1,0:T(8,128)(2,1)} %bitcast.38), channel_id=1, source_target_pairs={{0,4},{2,6},{4,0},{6,2},{1,5},{3,7},{5,1},{7,3},{8,12},{10,14},{12... | collective-permute-start | bytes 1769480 | tf_op jit(solution)/shard_map/ppermute | solution.py:291
  341.7 22.6 %collective-permute-start.19 = (bf16[256,1152]{1,0:T(8,128)(2,1)}, bf16[256,1152]{1,0:T(8,128)(2,1)}, u32[]{:S(2)}, u32[]{:S(2)}) collective-permute-start(bf16[256,1152]{1,0:T(8,128)(2,1)} %bitcast.36), channel_id=1, source_target_pairs={{0,4},{2,6},{4,0},{6,2},{1,5},{3,7},{5,1},{7,3},{8,12},{10,14},{12... | collective-permute-start | bytes 1769480 | tf_op jit(solution)/shard_map/ppermute | solution.py:291
  346.0 16.6 %collective-permute-start.17 = (bf16[256,1152]{1,0:T(8,128)(2,1)}, bf16[256,1152]{1,0:T(8,128)(2,1)}, u32[]{:S(2)}, u32[]{:S(2)}) collective-permute-start(bf16[256,1152]{1,0:T(8,128)(2,1)} %bitcast.34), channel_id=1, source_target_pairs={{0,2},{2,0},{4,6},{6,4},{1,3},{3,1},{5,7},{7,5},{8,10},{10,8},{12,... | collective-permute-start | bytes 1769480 | tf_op jit(solution)/shard_map/ppermute | solution.py:291
  346.3 40.4 %collective-permute-start.16 = (bf16[256,1152]{1,0:T(8,128)(2,1)}, bf16[256,1152]{1,0:T(8,128)(2,1)}, u32[]{:S(2)}, u32[]{:S(2)}) collective-permute-start(bf16[256,1152]{1,0:T(8,128)(2,1)} %bitcast.32), channel_id=1, source_target_pairs={{0,2},{2,0},{4,6},{6,4},{1,3},{3,1},{5,7},{7,5},{8,10},{10,8},{12,... | collective-permute-start | bytes 1769480 | tf_op jit(solution)/shard_map/ppermute | solution.py:291
  349.8 169.2 %reduce-scatter.7.cloned.1.call-start = ((), (), s32[]{:S(2)}) async-start(), calls=%async_computation.4 | async-start | bytes 1474560 | tf_op jit(solution)/shard_map/reduce_scatter | solution.py:333
  351.3 34.1 %collective-permute-start.21 = (bf16[256,1152]{1,0:T(8,128)(2,1)S(1)}, bf16[256,1152]{1,0:T(8,128)(2,1)S(1)}, u32[]{:S(2)}, u32[]{:S(2)}) collective-permute-start(bf16[256,1152]{1,0:T(8,128)(2,1)S(1)} %fusion.35), channel_id=1, source_target_pairs={{0,2},{2,0},{4,6},{6,4},{1,3},{3,1},{5,7},{7,5},{8,10},{10,8},{12,... | collective-permute-start | bytes 1769480 | tf_op jit(solution)/shard_map/ppermute | solution.py:291
  364.1 23.2 %collective-permute-start.18 = (bf16[256,1152]{1,0:T(8,128)(2,1)S(1)}, bf16[256,1152]{1,0:T(8,128)(2,1)S(1)}, u32[]{:S(2)}, u32[]{:S(2)}) collective-permute-start(bf16[256,1152]{1,0:T(8,128)(2,1)S(1)} %fusion.38), channel_id=1, source_target_pairs={{0,4},{2,6},{4,0},{6,2},{1,5},{3,7},{5,1},{7,3},{8,12},{10,14},{12... | collective-permute-start | bytes 1769480 | tf_op jit(solution)/shard_map/ppermute | solution.py:291
  364.3 27.8 %collective-permute-start.38 = (bf16[256,2048]{1,0:T(8,128)(2,1)S(1)}, bf16[256,2048]{1,0:T(8,128)(2,1)S(1)}, u32[]{:S(2)}, u32[]{:S(2)}) collective-permute-start(bf16[256,2048]{1,0:T(8,128)(2,1)S(1)} %copy-done.16), channel_id=1, source_target_pairs={{0,1},{1,0},{2,3},{3,2},{4,5},{5,4},{6,7},{7,6},{8,9},{9,8},{10,11... | collective-permute-start | bytes 3145736 | tf_op jit(solution)/shard_map/ppermute | solution.py:297
  385.4 7.8 %collective-permute-start.39 = (bf16[128,2048]{1,0:T(8,128)(2,1)}, bf16[128,2048]{1,0:T(8,128)(2,1)}, u32[]{:S(2)}, u32[]{:S(2)}) collective-permute-start(bf16[128,2048]{1,0:T(8,128)(2,1)} %collective-permute-done.35), channel_id=1, source_target_pairs={{0,1},{1,0},{2,3},{3,2},{4,5},{5,4},{6,7},{7,6},{8,9},{9,8},{10,11... | collective-permute-start | bytes 1572872 | tf_op jit(solution)/shard_map/ppermute | solution.py:297
  386.7 8.4 %collective-permute-start.40 = (bf16[128,2048]{1,0:T(8,128)(2,1)}, bf16[128,2048]{1,0:T(8,128)(2,1)}, u32[]{:S(2)}, u32[]{:S(2)}) collective-permute-start(bf16[128,2048]{1,0:T(8,128)(2,1)} %collective-permute-done.36), channel_id=1, source_target_pairs={{0,1},{1,0},{2,3},{3,2},{4,5},{5,4},{6,7},{7,6},{8,9},{9,8},{10,11... | collective-permute-start | bytes 1572872 | tf_op jit(solution)/shard_map/ppermute | solution.py:297
  389.7 133.5 %reduce-scatter.11.cloned.1.call-start = ((), (), s32[]{:S(2)}) async-start(), calls=%async_computation.6 | async-start | bytes 5242880 | tf_op jit(solution)/shard_map/reduce_scatter | solution.py:333
  426.0 166.2 %reduce-scatter.9.cloned.1.call-start = ((), (), s32[]{:S(2)}) async-start(), calls=%async_computation.5 | async-start | bytes 5242880 | tf_op jit(solution)/shard_map/reduce_scatter | solution.py:333
  455.2 39.1 %copy-start.4 = (bf16[1,512,2048]{2,1,0:T(8,128)(2,1)S(1)}, bf16[1,512,2048]{2,1,0:T(8,128)(2,1)}, u32[]{:S(2)}) copy-start(bf16[1,512,2048]{2,1,0:T(8,128)(2,1)} %param.17) | copy-start | bytes 6291460
  455.2 39.1 %copy-start.23 = (f32[2048]{0:T(1024)S(1)}, f32[2048]{0:T(1024)}, u32[]{:S(2)}) copy-start(f32[2048]{0:T(1024)} %param.19) | copy-start | bytes 24580
  455.2 39.1 %copy-start.25 = (f32[512]{0:T(512)S(1)}, f32[512]{0:T(512)}, u32[]{:S(2)}) copy-start(f32[512]{0:T(512)} %copy-done.24) | copy-start | bytes 6148
  461.6 32.7 %collective-permute-start.6 = (bf16[512,2048]{1,0:T(8,128)(2,1)}, bf16[512,2048]{1,0:T(8,128)(2,1)}, u32[]{:S(2)}, u32[]{:S(2)}) collective-permute-start(bf16[512,2048]{1,0:T(8,128)(2,1)} %convolution_convert_fusion.1), channel_id=1, source_target_pairs={{0,1},{1,0},{2,3},{3,2},{4,5},{5,4},{6,7},{7,6},{8,9},{9,8},{10,11... | collective-permute-start | bytes 6291464 | tf_op jit(solution)/shard_map/ppermute | solution.py:297
  461.7 4.2 collective-permute-start.29
  465.9 4.1 collective-permute-start.30
  470.0 6.4 %collective-permute-start.31 = (f32[12288]{0:T(1024)S(1)}, f32[12288]{0:T(1024)S(1)}, u32[]{:S(2)}, u32[]{:S(2)}) collective-permute-start(f32[12288]{0:T(1024)S(1)} %add.289), channel_id=1, source_target_pairs={{0,8},{8,0},{16,24},{24,16},{1,9},{9,1},{17,25},{25,17},{2,10},{10... | collective-permute-start | bytes 147464 | tf_op jit(solution)/shard_map/ppermute | solution.py:294
  476.5 17.7 %collective-permute-start.32 = (f32[12288]{0:T(1024)S(1)}, f32[12288]{0:T(1024)S(1)}, u32[]{:S(2)}, u32[]{:S(2)}) collective-permute-start(f32[12288]{0:T(1024)S(1)} %add.290), channel_id=1, source_target_pairs={{0,16},{8,24},{16,0},{24,8},{1,17},{9,25},{17,1},{25,9},{2,18},{10... | collective-permute-start | bytes 147464 | tf_op jit(solution)/shard_map/ppermute | solution.py:294
  487.5 6.6 %collective-permute-start.11 = (bf16[512,128]{1,0:T(8,128)(2,1)S(1)}, bf16[512,128]{1,0:T(8,128)(2,1)S(1)}, u32[]{:S(2)}, u32[]{:S(2)}) collective-permute-start(bf16[512,128]{1,0:T(8,128)(2,1)S(1)} %fusion.49), channel_id=1, source_target_pairs={{0,1},{1,0},{2,3},{3,2},{4,5},{5,4},{6,7},{7,6},{8,9},{9,8},{10,11... | collective-permute-start | bytes 393224 | tf_op jit(solution)/shard_map/ppermute | solution.py:297
  498.7 3.9 collective-permute-start.12
  502.6 3.8 collective-permute-start.13
  506.5 4.8 collective-permute-start.14
  511.3 4.8 collective-permute-start.15
  519.8 2.7 collective-permute-start.22
  594.5 12.1 %collective-permute-start.50 = (bf16[128,1024]{0,1:T(8,128)(2,1)}, bf16[128,1024]{0,1:T(8,128)(2,1)}, u32[]{:S(2)}, u32[]{:S(2)}) collective-permute-start(bf16[128,1024]{0,1:T(8,128)(2,1)} %bitcast.59), channel_id=1, source_target_pairs={{0,2},{2,0},{4,6},{6,4},{1,3},{3,1},{5,7},{7,5},{8,10},{10,8},{12,... | collective-permute-start | bytes 786440 | tf_op jit(solution)/shard_map/ppermute | solution.py:291
  596.8 12.8 %collective-permute-start.49 = (bf16[128,1024]{0,1:T(8,128)(2,1)}, bf16[128,1024]{0,1:T(8,128)(2,1)}, u32[]{:S(2)}, u32[]{:S(2)}) collective-permute-start(bf16[128,1024]{0,1:T(8,128)(2,1)} %bitcast.57), channel_id=1, source_target_pairs={{0,2},{2,0},{4,6},{6,4},{1,3},{3,1},{5,7},{7,5},{8,10},{10,8},{12,... | collective-permute-start | bytes 786440 | tf_op jit(solution)/shard_map/ppermute | solution.py:291
  599.1 11.7 %collective-permute-start.52 = (bf16[128,1024]{0,1:T(8,128)(2,1)}, bf16[128,1024]{0,1:T(8,128)(2,1)}, u32[]{:S(2)}, u32[]{:S(2)}) collective-permute-start(bf16[128,1024]{0,1:T(8,128)(2,1)} %bitcast.64), channel_id=1, source_target_pairs={{0,4},{2,6},{4,0},{6,2},{1,5},{3,7},{5,1},{7,3},{8,12},{10,14},{12... | collective-permute-start | bytes 786440 | tf_op jit(solution)/shard_map/ppermute | solution.py:291
  601.5 22.4 %collective-permute-start.51 = (bf16[128,1024]{0,1:T(8,128)(2,1)}, bf16[128,1024]{0,1:T(8,128)(2,1)}, u32[]{:S(2)}, u32[]{:S(2)}) collective-permute-start(bf16[128,1024]{0,1:T(8,128)(2,1)} %bitcast.62), channel_id=1, source_target_pairs={{0,4},{2,6},{4,0},{6,2},{1,5},{3,7},{5,1},{7,3},{8,12},{10,14},{12... | collective-permute-start | bytes 786440 | tf_op jit(solution)/shard_map/ppermute | solution.py:291
  602.2 23.6 %collective-permute-start.54 = (bf16[128,1024]{0,1:T(8,128)(2,1)S(1)}, bf16[128,1024]{0,1:T(8,128)(2,1)}, u32[]{:S(2)}, u32[]{:S(2)}) collective-permute-start(bf16[128,1024]{0,1:T(8,128)(2,1)S(1)} %bitcast.221), channel_id=1, source_target_pairs={{0,6},{2,4},{4,2},{6,0},{1,7},{3,5},{5,3},{7,1},{8,14},{10,12},{12... | collective-permute-start | bytes 786440 | tf_op jit(solution)/shard_map/ppermute | solution.py:291
  606.6 19.2 %collective-permute-start.53 = (bf16[128,1024]{0,1:T(8,128)(2,1)S(1)}, bf16[128,1024]{0,1:T(8,128)(2,1)S(1)}, u32[]{:S(2)}, u32[]{:S(2)}) collective-permute-start(bf16[128,1024]{0,1:T(8,128)(2,1)S(1)} %bitcast.222), channel_id=1, source_target_pairs={{0,6},{2,4},{4,2},{6,0},{1,7},{3,5},{5,3},{7,1},{8,14},{10,12},{12... | collective-permute-start | bytes 786440 | tf_op jit(solution)/shard_map/ppermute | solution.py:291
  (34 other events, 309.3 us)
Sparse Core Ops, SparseCore 0:
  349.9 34.2 reduce-scatter.12
  389.8 36.3 reduce-scatter.6
  428.6 83.9 reduce-scatter.10
  514.8 77.3 reduce-scatter.8
